TPU v7x, 512 devices: a whole 4x8x8 slice. The times are simulated.
512 devices in a mesh: seq: 64 (over x, y, core), dp: 8 (over z).
Axes of the slice: x: 4, y: 8, z: 8, core: 2. Of those that a mesh axis runs over, the one named last changes fastest.
Arguments:
- queries: bfloat16 [8, 8192, 512], P('dp', 'seq'), may hold values from -6 to 6
- keys: bfloat16 [8, 8192, 512], P('dp', 'seq'), may hold values from -6 to 6
- values: bfloat16 [8, 8192, 512], P('dp', 'seq'), may hold values from -6 to 6
- gates: bfloat16 [8, 8192, 512], P('dp', 'seq'), may hold values from -6 to 6
- cotangent: bfloat16 [8, 8192, 512], P('dp', 'seq'), may hold values from -6 to 6
- lengths: int32 [8, 5], P('dp'), may hold values from 1 to 32, 64 in all within a row
- gain: float32 [512], replicated, may hold values from 0.5 to 1.5
- bias: float32 [512], replicated, may hold values from -3 to 3
Outputs:
- grad_queries: bfloat16 [8, 8192, 512], P('dp', 'seq')
- grad_keys: bfloat16 [8, 8192, 512], P('dp', 'seq')
- grad_values: bfloat16 [8, 8192, 512], P('dp', 'seq')
- grad_gates: bfloat16 [8, 8192, 512], P('dp', 'seq')
- grad_gain: float32 [512], replicated
- grad_bias: float32 [512], replicated
Inputs may be any that keep to these rules, and one draw needn't show every extreme that they name: Each row of lengths sums to 64 and its largest entry is exactly 32; a user's last block holds a window of 128 of its candidates.
All inputs are finite; a program needn't handle non-finite values.
Results may differ from a plain program's by a relative error of at most 0.0058.
Values may be sent and summed in bfloat16 or wider, within the bound.
A program may use at most 64 MiB of HBM per device.

v0:
```python
import math

import jax
import jax.numpy as jnp
from jax import lax
from jax.sharding import PartitionSpec as P

HEADS = 4
HD = 128
BLOCK = 128


EPS = 1e-05


def passed_along(value, axis, steps):
    count = lax.axis_size(axis)
    first, last = (max(0, -steps), min(count, count - steps))
    return lax.ppermute(value, axis, [(source, source + steps) for source in range(first, last)])


def row_info(lengths, first, count, total):
    places = first + jnp.arange(count, dtype=jnp.int32)
    ends = jnp.cumsum(lengths)
    blocks = places // BLOCK
    owner = jnp.sum((blocks[:, None] >= ends[None, :]).astype(jnp.int32), axis=1)
    final = jnp.any(blocks[:, None] + 1 == ends[None, :], axis=1)
    inside = (places >= 0) & (places < total)
    owner = jnp.where(inside, owner, -1)
    return (owner, final, places)


def pair_mask(query_info, key_info):
    query_owner, query_final, query_rows = query_info
    key_owner, key_final, key_rows = key_info
    same = (query_owner[:, None] == key_owner[None, :]) & (query_owner[:, None] >= 0)
    causal = key_rows[None, :] <= query_rows[:, None]
    allowed = jnp.logical_not(key_final[None, :]) | (key_rows[None, :] == query_rows[:, None])
    return same & causal & allowed


def heads_of(block):
    return block.reshape(block.shape[0], HEADS, HD)


def scores_of(query_block, key_block):
    product = jnp.einsum(
        "qhd,khd->hqk",
        heads_of(query_block),
        heads_of(key_block),
        preferred_element_type=jnp.float32,
    )
    return product * HD ** (-0.5)


def forward_tile(query_block, key_block, value_block, mask):
    scores = scores_of(query_block, key_block)
    sigma = jax.nn.sigmoid(scores)
    probs = jnp.where(mask[None], scores * sigma, 0.0).astype(jnp.bfloat16)
    mixed = jnp.einsum(
        "hqk,khd->qhd", probs, heads_of(value_block), preferred_element_type=jnp.float32
    )
    return mixed.reshape(query_block.shape[0], -1)


def backward_tile(query_block, key_block, value_block, upstream, mask):
    scores = scores_of(query_block, key_block)
    sigma = jax.nn.sigmoid(scores)
    probs = jnp.where(mask[None], scores * sigma, 0.0).astype(jnp.bfloat16)
    deriv = sigma * (1.0 + scores * (1.0 - sigma))
    pressure = jnp.einsum(
        "qhd,khd->hqk",
        heads_of(upstream),
        heads_of(value_block),
        preferred_element_type=jnp.float32,
    )
    grad_scores = jnp.where(mask[None], pressure * deriv * HD ** (-0.5), 0.0).astype(jnp.bfloat16)
    return (grad_scores, probs)


def query_side(query_block, key_block, value_block, upstream, mask):
    grad_scores, probs = backward_tile(query_block, key_block, value_block, upstream, mask)
    grad_query = jnp.einsum(
        "hqk,khd->qhd", grad_scores, heads_of(key_block), preferred_element_type=jnp.float32
    )
    return grad_query.reshape(query_block.shape[0], -1)


def key_side(query_block, key_block, value_block, upstream, mask):
    grad_scores, probs = backward_tile(query_block, key_block, value_block, upstream, mask)
    grad_key = jnp.einsum(
        "hqk,qhd->khd", grad_scores, heads_of(query_block), preferred_element_type=jnp.float32
    )
    grad_value = jnp.einsum(
        "hqk,qhd->khd", probs, heads_of(upstream), preferred_element_type=jnp.float32
    )
    return (grad_key.reshape(key_block.shape[0], -1), grad_value.reshape(key_block.shape[0], -1))


def both_sides(query_block, key_block, value_block, upstream, mask):
    grad_scores, probs = backward_tile(query_block, key_block, value_block, upstream, mask)
    grad_query = jnp.einsum(
        "hqk,khd->qhd", grad_scores, heads_of(key_block), preferred_element_type=jnp.float32
    )
    grad_key = jnp.einsum(
        "hqk,qhd->khd", grad_scores, heads_of(query_block), preferred_element_type=jnp.float32
    )
    grad_value = jnp.einsum(
        "hqk,qhd->khd", probs, heads_of(upstream), preferred_element_type=jnp.float32
    )
    rows_query = query_block.shape[0]
    rows_key = key_block.shape[0]
    return (
        grad_query.reshape(rows_query, -1),
        grad_key.reshape(rows_key, -1),
        grad_value.reshape(rows_key, -1),
    )


def maybe_skip(function, operands):
    return function(*operands)


def per_device(queries, keys, values, gates, cotangent, lengths, gain, bias):
    query_local = queries[0]
    key_local = keys[0]
    value_local = values[0]
    user_lengths = lengths[0]
    tokens = query_local.shape[0]
    devices = lax.axis_size("seq")
    reach = devices // 2 - 1
    total = devices * tokens
    first = lax.axis_index("seq") * tokens
    own_info = row_info(user_lengths, first, tokens, total)
    distances = jnp.arange(1, reach + 1, dtype=jnp.int32)

    def near_mask(distance):
        return pair_mask(own_info, row_info(user_lengths, first - distance * tokens, tokens, total))

    own_mask = near_mask(0)
    attended = maybe_skip(forward_tile, (query_local, key_local, value_local, own_mask))

    def key_step(carry, distance):
        current, total_rows = carry
        current = passed_along((current[0], current[1]), "seq", 1)
        mask = near_mask(distance)
        total_rows = total_rows + maybe_skip(
            forward_tile, (query_local, current[0], current[1], mask)
        )
        return ((current, total_rows), current)

    (last_pair, attended), stored = lax.scan(
        key_step, ((key_local, value_local), attended), distances
    )
    stored_keys, stored_values = stored
    mean = jnp.mean(attended, axis=-1, keepdims=True)
    centered = attended - mean
    variance = jnp.mean(centered * centered, axis=-1, keepdims=True)
    inverse = lax.rsqrt(variance + EPS)
    normal = centered * inverse
    scaled = normal * gain + bias
    cot_float = cotangent[0].astype(jnp.float32)
    upstream_norm = cot_float * gates[0].astype(jnp.float32)
    grad_gates = (cot_float * scaled).astype(jnp.bfloat16)
    gain_sum, bias_sum = lax.psum(
        (jnp.sum(upstream_norm * normal, axis=0), jnp.sum(upstream_norm, axis=0)), ("seq", "dp")
    )
    norm_scale = 1.0 / math.sqrt(lax.axis_size("dp") * total)
    dnormal = upstream_norm * gain
    grad_attended = inverse * (
        dnormal
        - jnp.mean(dnormal, axis=-1, keepdims=True)
        - normal * jnp.mean(dnormal * normal, axis=-1, keepdims=True)
    )
    upstream = grad_attended.astype(jnp.bfloat16)
    grad_query, grad_key, grad_value = maybe_skip(
        both_sides, (query_local, key_local, value_local, upstream, own_mask)
    )

    def back_step(carry, items):
        current, sum_query, sum_key, sum_value = carry
        distance, key_block, value_block = items
        current = passed_along((current[0], current[1]), "seq", -1)
        mask = near_mask(distance)
        sum_query = sum_query + maybe_skip(
            query_side, (query_local, key_block, value_block, upstream, mask)
        )
        far_mask = pair_mask(
            row_info(user_lengths, first + distance * tokens, tokens, total), own_info
        )
        part_key, part_value = maybe_skip(
            key_side, (current[0], key_local, value_local, current[1], far_mask)
        )
        return ((current, sum_query, sum_key + part_key, sum_value + part_value), None)

    (last_queries, grad_query, grad_key, grad_value), unused_back = lax.scan(
        back_step,
        ((query_local, upstream), grad_query, grad_key, grad_value),
        (distances, stored_keys, stored_values),
    )
    return (
        grad_query.astype(jnp.bfloat16)[None],
        grad_key.astype(jnp.bfloat16)[None],
        grad_value.astype(jnp.bfloat16)[None],
        grad_gates[None],
        gain_sum * norm_scale,
        bias_sum * norm_scale,
    )


def solution(mesh):
    in_specs = (
        P("dp", "seq", None),
        P("dp", "seq", None),
        P("dp", "seq", None),
        P("dp", "seq", None),
        P("dp", "seq", None),
        P("dp", None),
        P(),
        P(),
    )
    out_specs = (
        P("dp", "seq", None),
        P("dp", "seq", None),
        P("dp", "seq", None),
        P("dp", "seq", None),
        P(),
        P(),
    )
    return jax.shard_map(
        per_device, mesh=mesh, in_specs=in_specs, out_specs=out_specs, check_vma=False
    )
```

profile of v0, /device:TPU:3, one launch (start us, length us, event | category | flops | bytes accessed | tf_op | source)
XLA Modules:
  0.0 833.0 jit_solution(9761001088353409769)
XLA Ops:
  8.2 370.3 %while.47 = (s32[]{:T(128)}, bf16[128,512]{0,1:T(8,128)(2,1)S(1)}, bf16[128,512]{0,1:T(8,128)(2,1)S(1)}, f32[128,512]{0,1:T(8,128)S(1)}, bf16[31,128,512]{1,2,0:...) while((s32[]{:T(128)}, bf16[128,512]{0,1:T(8,128)(2,1)S(1)}, ...), condition=%wide.wide.region_7.8_spmd.clone.clone, body=%wide.wide.region_4.7_spmd.clone.clone.sunk | while | flops 34199684 | bytes 3579969 | solution.py:152
  8.2 3.9 collective-permute-start.1
  17.8 4.3 collective-permute-start.1
  27.7 4.3 collective-permute-start.1
  57.2 2.9 collective-permute-done.1
  81.4 2.9 collective-permute-done.1
  105.6 2.9 collective-permute-done.1
  141.9 2.9 collective-permute-done.1
  166.2 2.9 collective-permute-done.1
  178.3 2.9 collective-permute-done.1
  202.5 2.9 collective-permute-done.1
  226.7 2.9 collective-permute-done.1
  238.8 2.9 collective-permute-done.1
  250.9 2.9 collective-permute-done.1
  311.4 2.9 collective-permute-done.1
  335.6 2.9 collective-permute-done.1
  379.8 106.7 %all-reduce = (f32[512]{0:T(512)S(1)}, f32[512]{0:T(512)S(1)}) all-reduce(f32[512]{0:T(512)S(1)} %get-tuple-element.653, f32[512]{0:T(512)S(1)} %get-tuple-element.656), channel_id=1, replica_groups=mesh['seq'=64,'dp'=8] {'seq','dp'}, use_global_device_ids=true, to_apply=%region_18.19 | all-reduce | flops 1024 | bytes 8192 | tf_op jit(solution)/shard_map/psum | solution.py:165
  489.0 341.8 %while.48 = (s32[]{:T(128)}, bf16[128,512]{0,1:T(8,128)(2,1)S(1)}, bf16[128,512]{0,1:T(8,128)(2,1)S(1)}, f32[128,512]{0,1:T(8,128)S(1)}, f32[128,512]{0,1:T(8,12...) while((s32[]{:T(128)}, bf16[128,512]{0,1:T(8,128)(2,1)S(1)}, ...), condition=%wide.wide.region_16.17_spmd.clone.clone, body=%wide.wide.region_12.16_spmd.clone.clone.sunk | while | flops 119845632 | bytes 8090137 | solution.py:196
  501.1 4.8 collective-permute-start.3
  512.1 4.8 collective-permute-start.3
  523.2 4.8 collective-permute-start.3
  534.2 4.8 collective-permute-start.3
  545.3 4.8 collective-permute-start.3
  556.3 4.8 collective-permute-start.3
  567.4 4.8 collective-permute-start.3
  578.4 4.8 collective-permute-start.3
  589.5 4.8 collective-permute-start.3
  600.5 4.8 collective-permute-start.3
  611.6 4.8 collective-permute-start.3
  622.7 4.8 collective-permute-start.3
  633.7 4.8 collective-permute-start.3
  644.8 4.8 collective-permute-start.3
  655.8 4.8 collective-permute-start.3
  666.9 4.8 collective-permute-start.3
  677.9 4.8 collective-permute-start.3
  689.0 4.8 collective-permute-start.3
  700.0 4.8 collective-permute-start.3
  711.1 4.8 collective-permute-start.3
  722.1 4.8 collective-permute-start.3
  733.2 4.8 collective-permute-start.3
  744.3 4.8 collective-permute-start.3
  755.3 4.8 collective-permute-start.3
  766.4 4.8 collective-permute-start.3
  777.4 4.8 collective-permute-start.3
  788.5 4.8 collective-permute-start.3
  799.5 4.8 collective-permute-start.3
  810.6 4.8 collective-permute-start.3
  821.6 4.8 collective-permute-start.3
  (1468 shorter events, 485.6 us)
Async XLA Ops:
  53.7 8.4 %collective-permute-start = (bf16[128,512]{0,1:T(8,128)(2,1)S(1)}, bf16[128,512]{0,1:T(8,128)(2,1)S(1)}, u32[]{:S(2)}, u32[]{:S(2)}) collective-permute-start(bf16[128,512]{0,1:T(8,128)(2,1)S(1)} %get-tuple-element.1095), channel_id=1, source_target_pairs={{0,8},{8,16},{16,24},{24,32},{32,40},{40,48},{48,56},{56,64},{64,7... | collective-permute-start | bytes 393224 | tf_op jit(solution)/shard_map/while/body/eval_jaxpr/ppermute | solution.py:19
  77.9 8.4 %collective-permute-start = (bf16[128,512]{0,1:T(8,128)(2,1)S(1)}, bf16[128,512]{0,1:T(8,128)(2,1)S(1)}, u32[]{:S(2)}, u32[]{:S(2)}) collective-permute-start(bf16[128,512]{0,1:T(8,128)(2,1)S(1)} %get-tuple-element.1095), channel_id=1, source_target_pairs={{0,8},{8,16},{16,24},{24,32},{32,40},{40,48},{48,56},{56,64},{64,7... | collective-permute-start | bytes 393224 | tf_op jit(solution)/shard_map/while/body/eval_jaxpr/ppermute | solution.py:19
  90.0 8.4 %collective-permute-start = (bf16[128,512]{0,1:T(8,128)(2,1)S(1)}, bf16[128,512]{0,1:T(8,128)(2,1)S(1)}, u32[]{:S(2)}, u32[]{:S(2)}) collective-permute-start(bf16[128,512]{0,1:T(8,128)(2,1)S(1)} %get-tuple-element.1095), channel_id=1, source_target_pairs={{0,8},{8,16},{16,24},{24,32},{32,40},{40,48},{48,56},{56,64},{64,7... | collective-permute-start | bytes 393224 | tf_op jit(solution)/shard_map/while/body/eval_jaxpr/ppermute | solution.py:19
  102.1 8.4 %collective-permute-start = (bf16[128,512]{0,1:T(8,128)(2,1)S(1)}, bf16[128,512]{0,1:T(8,128)(2,1)S(1)}, u32[]{:S(2)}, u32[]{:S(2)}) collective-permute-start(bf16[128,512]{0,1:T(8,128)(2,1)S(1)} %get-tuple-element.1095), channel_id=1, source_target_pairs={{0,8},{8,16},{16,24},{24,32},{32,40},{40,48},{48,56},{56,64},{64,7... | collective-permute-start | bytes 393224 | tf_op jit(solution)/shard_map/while/body/eval_jaxpr/ppermute | solution.py:19
  114.2 8.4 %collective-permute-start = (bf16[128,512]{0,1:T(8,128)(2,1)S(1)}, bf16[128,512]{0,1:T(8,128)(2,1)S(1)}, u32[]{:S(2)}, u32[]{:S(2)}) collective-permute-start(bf16[128,512]{0,1:T(8,128)(2,1)S(1)} %get-tuple-element.1095), channel_id=1, source_target_pairs={{0,8},{8,16},{16,24},{24,32},{32,40},{40,48},{48,56},{56,64},{64,7... | collective-permute-start | bytes 393224 | tf_op jit(solution)/shard_map/while/body/eval_jaxpr/ppermute | solution.py:19
  138.4 8.4 %collective-permute-start = (bf16[128,512]{0,1:T(8,128)(2,1)S(1)}, bf16[128,512]{0,1:T(8,128)(2,1)S(1)}, u32[]{:S(2)}, u32[]{:S(2)}) collective-permute-start(bf16[128,512]{0,1:T(8,128)(2,1)S(1)} %get-tuple-element.1095), channel_id=1, source_target_pairs={{0,8},{8,16},{16,24},{24,32},{32,40},{40,48},{48,56},{56,64},{64,7... | collective-permute-start | bytes 393224 | tf_op jit(solution)/shard_map/while/body/eval_jaxpr/ppermute | solution.py:19
  162.6 8.4 %collective-permute-start = (bf16[128,512]{0,1:T(8,128)(2,1)S(1)}, bf16[128,512]{0,1:T(8,128)(2,1)S(1)}, u32[]{:S(2)}, u32[]{:S(2)}) collective-permute-start(bf16[128,512]{0,1:T(8,128)(2,1)S(1)} %get-tuple-element.1095), channel_id=1, source_target_pairs={{0,8},{8,16},{16,24},{24,32},{32,40},{40,48},{48,56},{56,64},{64,7... | collective-permute-start | bytes 393224 | tf_op jit(solution)/shard_map/while/body/eval_jaxpr/ppermute | solution.py:19
  174.7 8.4 %collective-permute-start = (bf16[128,512]{0,1:T(8,128)(2,1)S(1)}, bf16[128,512]{0,1:T(8,128)(2,1)S(1)}, u32[]{:S(2)}, u32[]{:S(2)}) collective-permute-start(bf16[128,512]{0,1:T(8,128)(2,1)S(1)} %get-tuple-element.1095), channel_id=1, source_target_pairs={{0,8},{8,16},{16,24},{24,32},{32,40},{40,48},{48,56},{56,64},{64,7... | collective-permute-start | bytes 393224 | tf_op jit(solution)/shard_map/while/body/eval_jaxpr/ppermute | solution.py:19
  199.0 8.4 %collective-permute-start = (bf16[128,512]{0,1:T(8,128)(2,1)S(1)}, bf16[128,512]{0,1:T(8,128)(2,1)S(1)}, u32[]{:S(2)}, u32[]{:S(2)}) collective-permute-start(bf16[128,512]{0,1:T(8,128)(2,1)S(1)} %get-tuple-element.1095), channel_id=1, source_target_pairs={{0,8},{8,16},{16,24},{24,32},{32,40},{40,48},{48,56},{56,64},{64,7... | collective-permute-start | bytes 393224 | tf_op jit(solution)/shard_map/while/body/eval_jaxpr/ppermute | solution.py:19
  223.2 8.4 %collective-permute-start = (bf16[128,512]{0,1:T(8,128)(2,1)S(1)}, bf16[128,512]{0,1:T(8,128)(2,1)S(1)}, u32[]{:S(2)}, u32[]{:S(2)}) collective-permute-start(bf16[128,512]{0,1:T(8,128)(2,1)S(1)} %get-tuple-element.1095), channel_id=1, source_target_pairs={{0,8},{8,16},{16,24},{24,32},{32,40},{40,48},{48,56},{56,64},{64,7... | collective-permute-start | bytes 393224 | tf_op jit(solution)/shard_map/while/body/eval_jaxpr/ppermute | solution.py:19
  235.3 8.4 %collective-permute-start = (bf16[128,512]{0,1:T(8,128)(2,1)S(1)}, bf16[128,512]{0,1:T(8,128)(2,1)S(1)}, u32[]{:S(2)}, u32[]{:S(2)}) collective-permute-start(bf16[128,512]{0,1:T(8,128)(2,1)S(1)} %get-tuple-element.1095), channel_id=1, source_target_pairs={{0,8},{8,16},{16,24},{24,32},{32,40},{40,48},{48,56},{56,64},{64,7... | collective-permute-start | bytes 393224 | tf_op jit(solution)/shard_map/while/body/eval_jaxpr/ppermute | solution.py:19
  247.4 8.4 %collective-permute-start = (bf16[128,512]{0,1:T(8,128)(2,1)S(1)}, bf16[128,512]{0,1:T(8,128)(2,1)S(1)}, u32[]{:S(2)}, u32[]{:S(2)}) collective-permute-start(bf16[128,512]{0,1:T(8,128)(2,1)S(1)} %get-tuple-element.1095), channel_id=1, source_target_pairs={{0,8},{8,16},{16,24},{24,32},{32,40},{40,48},{48,56},{56,64},{64,7... | collective-permute-start | bytes 393224 | tf_op jit(solution)/shard_map/while/body/eval_jaxpr/ppermute | solution.py:19
  271.6 8.4 %collective-permute-start = (bf16[128,512]{0,1:T(8,128)(2,1)S(1)}, bf16[128,512]{0,1:T(8,128)(2,1)S(1)}, u32[]{:S(2)}, u32[]{:S(2)}) collective-permute-start(bf16[128,512]{0,1:T(8,128)(2,1)S(1)} %get-tuple-element.1095), channel_id=1, source_target_pairs={{0,8},{8,16},{16,24},{24,32},{32,40},{40,48},{48,56},{56,64},{64,7... | collective-permute-start | bytes 393224 | tf_op jit(solution)/shard_map/while/body/eval_jaxpr/ppermute | solution.py:19
  295.7 8.4 %collective-permute-start = (bf16[128,512]{0,1:T(8,128)(2,1)S(1)}, bf16[128,512]{0,1:T(8,128)(2,1)S(1)}, u32[]{:S(2)}, u32[]{:S(2)}) collective-permute-start(bf16[128,512]{0,1:T(8,128)(2,1)S(1)} %get-tuple-element.1095), channel_id=1, source_target_pairs={{0,8},{8,16},{16,24},{24,32},{32,40},{40,48},{48,56},{56,64},{64,7... | collective-permute-start | bytes 393224 | tf_op jit(solution)/shard_map/while/body/eval_jaxpr/ppermute | solution.py:19
  307.9 8.4 %collective-permute-start = (bf16[128,512]{0,1:T(8,128)(2,1)S(1)}, bf16[128,512]{0,1:T(8,128)(2,1)S(1)}, u32[]{:S(2)}, u32[]{:S(2)}) collective-permute-start(bf16[128,512]{0,1:T(8,128)(2,1)S(1)} %get-tuple-element.1095), channel_id=1, source_target_pairs={{0,8},{8,16},{16,24},{24,32},{32,40},{40,48},{48,56},{56,64},{64,7... | collective-permute-start | bytes 393224 | tf_op jit(solution)/shard_map/while/body/eval_jaxpr/ppermute | solution.py:19
  332.1 8.4 %collective-permute-start = (bf16[128,512]{0,1:T(8,128)(2,1)S(1)}, bf16[128,512]{0,1:T(8,128)(2,1)S(1)}, u32[]{:S(2)}, u32[]{:S(2)}) collective-permute-start(bf16[128,512]{0,1:T(8,128)(2,1)S(1)} %get-tuple-element.1095), channel_id=1, source_target_pairs={{0,8},{8,16},{16,24},{24,32},{32,40},{40,48},{48,56},{56,64},{64,7... | collective-permute-start | bytes 393224 | tf_op jit(solution)/shard_map/while/body/eval_jaxpr/ppermute | solution.py:19
  344.2 8.4 %collective-permute-start = (bf16[128,512]{0,1:T(8,128)(2,1)S(1)}, bf16[128,512]{0,1:T(8,128)(2,1)S(1)}, u32[]{:S(2)}, u32[]{:S(2)}) collective-permute-start(bf16[128,512]{0,1:T(8,128)(2,1)S(1)} %get-tuple-element.1095), channel_id=1, source_target_pairs={{0,8},{8,16},{16,24},{24,32},{32,40},{40,48},{48,56},{56,64},{64,7... | collective-permute-start | bytes 393224 | tf_op jit(solution)/shard_map/while/body/eval_jaxpr/ppermute | solution.py:19
  489.0 8.5 %collective-permute-start.2 = (bf16[128,512]{0,1:T(8,128)(2,1)S(1)}, bf16[128,512]{0,1:T(8,128)(2,1)S(1)}, u32[]{:S(2)}, u32[]{:S(2)}) collective-permute-start(bf16[128,512]{0,1:T(8,128)(2,1)S(1)} %get-tuple-element.1145), channel_id=1, source_target_pairs={{8,0},{16,8},{24,16},{32,24},{40,32},{48,40},{56,48},{64,56},{72,6... | collective-permute-start | bytes 393224 | tf_op jit(solution)/shard_map/while/body/eval_jaxpr/ppermute | solution.py:19
  498.9 10.4 %collective-permute-start.2 = (bf16[128,512]{0,1:T(8,128)(2,1)S(1)}, bf16[128,512]{0,1:T(8,128)(2,1)S(1)}, u32[]{:S(2)}, u32[]{:S(2)}) collective-permute-start(bf16[128,512]{0,1:T(8,128)(2,1)S(1)} %get-tuple-element.1145), channel_id=1, source_target_pairs={{8,0},{16,8},{24,16},{32,24},{40,32},{48,40},{56,48},{64,56},{72,6... | collective-permute-start | bytes 393224 | tf_op jit(solution)/shard_map/while/body/eval_jaxpr/ppermute | solution.py:19
  510.2 10.1 %collective-permute-start.2 = (bf16[128,512]{0,1:T(8,128)(2,1)S(1)}, bf16[128,512]{0,1:T(8,128)(2,1)S(1)}, u32[]{:S(2)}, u32[]{:S(2)}) collective-permute-start(bf16[128,512]{0,1:T(8,128)(2,1)S(1)} %get-tuple-element.1145), channel_id=1, source_target_pairs={{8,0},{16,8},{24,16},{32,24},{40,32},{48,40},{56,48},{64,56},{72,6... | collective-permute-start | bytes 393224 | tf_op jit(solution)/shard_map/while/body/eval_jaxpr/ppermute | solution.py:19
  521.2 10.1 %collective-permute-start.2 = (bf16[128,512]{0,1:T(8,128)(2,1)S(1)}, bf16[128,512]{0,1:T(8,128)(2,1)S(1)}, u32[]{:S(2)}, u32[]{:S(2)}) collective-permute-start(bf16[128,512]{0,1:T(8,128)(2,1)S(1)} %get-tuple-element.1145), channel_id=1, source_target_pairs={{8,0},{16,8},{24,16},{32,24},{40,32},{48,40},{56,48},{64,56},{72,6... | collective-permute-start | bytes 393224 | tf_op jit(solution)/shard_map/while/body/eval_jaxpr/ppermute | solution.py:19
  532.3 10.1 %collective-permute-start.2 = (bf16[128,512]{0,1:T(8,128)(2,1)S(1)}, bf16[128,512]{0,1:T(8,128)(2,1)S(1)}, u32[]{:S(2)}, u32[]{:S(2)}) collective-permute-start(bf16[128,512]{0,1:T(8,128)(2,1)S(1)} %get-tuple-element.1145), channel_id=1, source_target_pairs={{8,0},{16,8},{24,16},{32,24},{40,32},{48,40},{56,48},{64,56},{72,6... | collective-permute-start | bytes 393224 | tf_op jit(solution)/shard_map/while/body/eval_jaxpr/ppermute | solution.py:19
  543.3 10.1 %collective-permute-start.2 = (bf16[128,512]{0,1:T(8,128)(2,1)S(1)}, bf16[128,512]{0,1:T(8,128)(2,1)S(1)}, u32[]{:S(2)}, u32[]{:S(2)}) collective-permute-start(bf16[128,512]{0,1:T(8,128)(2,1)S(1)} %get-tuple-element.1145), channel_id=1, source_target_pairs={{8,0},{16,8},{24,16},{32,24},{40,32},{48,40},{56,48},{64,56},{72,6... | collective-permute-start | bytes 393224 | tf_op jit(solution)/shard_map/while/body/eval_jaxpr/ppermute | solution.py:19
  554.4 10.1 %collective-permute-start.2 = (bf16[128,512]{0,1:T(8,128)(2,1)S(1)}, bf16[128,512]{0,1:T(8,128)(2,1)S(1)}, u32[]{:S(2)}, u32[]{:S(2)}) collective-permute-start(bf16[128,512]{0,1:T(8,128)(2,1)S(1)} %get-tuple-element.1145), channel_id=1, source_target_pairs={{8,0},{16,8},{24,16},{32,24},{40,32},{48,40},{56,48},{64,56},{72,6... | collective-permute-start | bytes 393224 | tf_op jit(solution)/shard_map/while/body/eval_jaxpr/ppermute | solution.py:19
  565.5 10.1 %collective-permute-start.2 = (bf16[128,512]{0,1:T(8,128)(2,1)S(1)}, bf16[128,512]{0,1:T(8,128)(2,1)S(1)}, u32[]{:S(2)}, u32[]{:S(2)}) collective-permute-start(bf16[128,512]{0,1:T(8,128)(2,1)S(1)} %get-tuple-element.1145), channel_id=1, source_target_pairs={{8,0},{16,8},{24,16},{32,24},{40,32},{48,40},{56,48},{64,56},{72,6... | collective-permute-start | bytes 393224 | tf_op jit(solution)/shard_map/while/body/eval_jaxpr/ppermute | solution.py:19
  576.5 10.1 %collective-permute-start.2 = (bf16[128,512]{0,1:T(8,128)(2,1)S(1)}, bf16[128,512]{0,1:T(8,128)(2,1)S(1)}, u32[]{:S(2)}, u32[]{:S(2)}) collective-permute-start(bf16[128,512]{0,1:T(8,128)(2,1)S(1)} %get-tuple-element.1145), channel_id=1, source_target_pairs={{8,0},{16,8},{24,16},{32,24},{40,32},{48,40},{56,48},{64,56},{72,6... | collective-permute-start | bytes 393224 | tf_op jit(solution)/shard_map/while/body/eval_jaxpr/ppermute | solution.py:19
  587.6 10.1 %collective-permute-start.2 = (bf16[128,512]{0,1:T(8,128)(2,1)S(1)}, bf16[128,512]{0,1:T(8,128)(2,1)S(1)}, u32[]{:S(2)}, u32[]{:S(2)}) collective-permute-start(bf16[128,512]{0,1:T(8,128)(2,1)S(1)} %get-tuple-element.1145), channel_id=1, source_target_pairs={{8,0},{16,8},{24,16},{32,24},{40,32},{48,40},{56,48},{64,56},{72,6... | collective-permute-start | bytes 393224 | tf_op jit(solution)/shard_map/while/body/eval_jaxpr/ppermute | solution.py:19
  598.6 10.1 %collective-permute-start.2 = (bf16[128,512]{0,1:T(8,128)(2,1)S(1)}, bf16[128,512]{0,1:T(8,128)(2,1)S(1)}, u32[]{:S(2)}, u32[]{:S(2)}) collective-permute-start(bf16[128,512]{0,1:T(8,128)(2,1)S(1)} %get-tuple-element.1145), channel_id=1, source_target_pairs={{8,0},{16,8},{24,16},{32,24},{40,32},{48,40},{56,48},{64,56},{72,6... | collective-permute-start | bytes 393224 | tf_op jit(solution)/shard_map/while/body/eval_jaxpr/ppermute | solution.py:19
  609.7 10.1 %collective-permute-start.2 = (bf16[128,512]{0,1:T(8,128)(2,1)S(1)}, bf16[128,512]{0,1:T(8,128)(2,1)S(1)}, u32[]{:S(2)}, u32[]{:S(2)}) collective-permute-start(bf16[128,512]{0,1:T(8,128)(2,1)S(1)} %get-tuple-element.1145), channel_id=1, source_target_pairs={{8,0},{16,8},{24,16},{32,24},{40,32},{48,40},{56,48},{64,56},{72,6... | collective-permute-start | bytes 393224 | tf_op jit(solution)/shard_map/while/body/eval_jaxpr/ppermute | solution.py:19
  620.7 10.1 %collective-permute-start.2 = (bf16[128,512]{0,1:T(8,128)(2,1)S(1)}, bf16[128,512]{0,1:T(8,128)(2,1)S(1)}, u32[]{:S(2)}, u32[]{:S(2)}) collective-permute-start(bf16[128,512]{0,1:T(8,128)(2,1)S(1)} %get-tuple-element.1145), channel_id=1, source_target_pairs={{8,0},{16,8},{24,16},{32,24},{40,32},{48,40},{56,48},{64,56},{72,6... | collective-permute-start | bytes 393224 | tf_op jit(solution)/shard_map/while/body/eval_jaxpr/ppermute | solution.py:19
  631.8 10.1 %collective-permute-start.2 = (bf16[128,512]{0,1:T(8,128)(2,1)S(1)}, bf16[128,512]{0,1:T(8,128)(2,1)S(1)}, u32[]{:S(2)}, u32[]{:S(2)}) collective-permute-start(bf16[128,512]{0,1:T(8,128)(2,1)S(1)} %get-tuple-element.1145), channel_id=1, source_target_pairs={{8,0},{16,8},{24,16},{32,24},{40,32},{48,40},{56,48},{64,56},{72,6... | collective-permute-start | bytes 393224 | tf_op jit(solution)/shard_map/while/body/eval_jaxpr/ppermute | solution.py:19
  642.8 10.1 %collective-permute-start.2 = (bf16[128,512]{0,1:T(8,128)(2,1)S(1)}, bf16[128,512]{0,1:T(8,128)(2,1)S(1)}, u32[]{:S(2)}, u32[]{:S(2)}) collective-permute-start(bf16[128,512]{0,1:T(8,128)(2,1)S(1)} %get-tuple-element.1145), channel_id=1, source_target_pairs={{8,0},{16,8},{24,16},{32,24},{40,32},{48,40},{56,48},{64,56},{72,6... | collective-permute-start | bytes 393224 | tf_op jit(solution)/shard_map/while/body/eval_jaxpr/ppermute | solution.py:19
  653.9 10.1 %collective-permute-start.2 = (bf16[128,512]{0,1:T(8,128)(2,1)S(1)}, bf16[128,512]{0,1:T(8,128)(2,1)S(1)}, u32[]{:S(2)}, u32[]{:S(2)}) collective-permute-start(bf16[128,512]{0,1:T(8,128)(2,1)S(1)} %get-tuple-element.1145), channel_id=1, source_target_pairs={{8,0},{16,8},{24,16},{32,24},{40,32},{48,40},{56,48},{64,56},{72,6... | collective-permute-start | bytes 393224 | tf_op jit(solution)/shard_map/while/body/eval_jaxpr/ppermute | solution.py:19
  664.9 10.1 %collective-permute-start.2 = (bf16[128,512]{0,1:T(8,128)(2,1)S(1)}, bf16[128,512]{0,1:T(8,128)(2,1)S(1)}, u32[]{:S(2)}, u32[]{:S(2)}) collective-permute-start(bf16[128,512]{0,1:T(8,128)(2,1)S(1)} %get-tuple-element.1145), channel_id=1, source_target_pairs={{8,0},{16,8},{24,16},{32,24},{40,32},{48,40},{56,48},{64,56},{72,6... | collective-permute-start | bytes 393224 | tf_op jit(solution)/shard_map/while/body/eval_jaxpr/ppermute | solution.py:19
  676.0 10.1 %collective-permute-start.2 = (bf16[128,512]{0,1:T(8,128)(2,1)S(1)}, bf16[128,512]{0,1:T(8,128)(2,1)S(1)}, u32[]{:S(2)}, u32[]{:S(2)}) collective-permute-start(bf16[128,512]{0,1:T(8,128)(2,1)S(1)} %get-tuple-element.1145), channel_id=1, source_target_pairs={{8,0},{16,8},{24,16},{32,24},{40,32},{48,40},{56,48},{64,56},{72,6... | collective-permute-start | bytes 393224 | tf_op jit(solution)/shard_map/while/body/eval_jaxpr/ppermute | solution.py:19
  687.1 10.1 %collective-permute-start.2 = (bf16[128,512]{0,1:T(8,128)(2,1)S(1)}, bf16[128,512]{0,1:T(8,128)(2,1)S(1)}, u32[]{:S(2)}, u32[]{:S(2)}) collective-permute-start(bf16[128,512]{0,1:T(8,128)(2,1)S(1)} %get-tuple-element.1145), channel_id=1, source_target_pairs={{8,0},{16,8},{24,16},{32,24},{40,32},{48,40},{56,48},{64,56},{72,6... | collective-permute-start | bytes 393224 | tf_op jit(solution)/shard_map/while/body/eval_jaxpr/ppermute | solution.py:19
  698.1 10.1 %collective-permute-start.2 = (bf16[128,512]{0,1:T(8,128)(2,1)S(1)}, bf16[128,512]{0,1:T(8,128)(2,1)S(1)}, u32[]{:S(2)}, u32[]{:S(2)}) collective-permute-start(bf16[128,512]{0,1:T(8,128)(2,1)S(1)} %get-tuple-element.1145), channel_id=1, source_target_pairs={{8,0},{16,8},{24,16},{32,24},{40,32},{48,40},{56,48},{64,56},{72,6... | collective-permute-start | bytes 393224 | tf_op jit(solution)/shard_map/while/body/eval_jaxpr/ppermute | solution.py:19
  709.2 10.1 %collective-permute-start.2 = (bf16[128,512]{0,1:T(8,128)(2,1)S(1)}, bf16[128,512]{0,1:T(8,128)(2,1)S(1)}, u32[]{:S(2)}, u32[]{:S(2)}) collective-permute-start(bf16[128,512]{0,1:T(8,128)(2,1)S(1)} %get-tuple-element.1145), channel_id=1, source_target_pairs={{8,0},{16,8},{24,16},{32,24},{40,32},{48,40},{56,48},{64,56},{72,6... | collective-permute-start | bytes 393224 | tf_op jit(solution)/shard_map/while/body/eval_jaxpr/ppermute | solution.py:19
  720.2 10.1 %collective-permute-start.2 = (bf16[128,512]{0,1:T(8,128)(2,1)S(1)}, bf16[128,512]{0,1:T(8,128)(2,1)S(1)}, u32[]{:S(2)}, u32[]{:S(2)}) collective-permute-start(bf16[128,512]{0,1:T(8,128)(2,1)S(1)} %get-tuple-element.1145), channel_id=1, source_target_pairs={{8,0},{16,8},{24,16},{32,24},{40,32},{48,40},{56,48},{64,56},{72,6... | collective-permute-start | bytes 393224 | tf_op jit(solution)/shard_map/while/body/eval_jaxpr/ppermute | solution.py:19
  731.3 10.1 %collective-permute-start.2 = (bf16[128,512]{0,1:T(8,128)(2,1)S(1)}, bf16[128,512]{0,1:T(8,128)(2,1)S(1)}, u32[]{:S(2)}, u32[]{:S(2)}) collective-permute-start(bf16[128,512]{0,1:T(8,128)(2,1)S(1)} %get-tuple-element.1145), channel_id=1, source_target_pairs={{8,0},{16,8},{24,16},{32,24},{40,32},{48,40},{56,48},{64,56},{72,6... | collective-permute-start | bytes 393224 | tf_op jit(solution)/shard_map/while/body/eval_jaxpr/ppermute | solution.py:19
  742.3 10.1 %collective-permute-start.2 = (bf16[128,512]{0,1:T(8,128)(2,1)S(1)}, bf16[128,512]{0,1:T(8,128)(2,1)S(1)}, u32[]{:S(2)}, u32[]{:S(2)}) collective-permute-start(bf16[128,512]{0,1:T(8,128)(2,1)S(1)} %get-tuple-element.1145), channel_id=1, source_target_pairs={{8,0},{16,8},{24,16},{32,24},{40,32},{48,40},{56,48},{64,56},{72,6... | collective-permute-start | bytes 393224 | tf_op jit(solution)/shard_map/while/body/eval_jaxpr/ppermute | solution.py:19
  753.4 10.1 %collective-permute-start.2 = (bf16[128,512]{0,1:T(8,128)(2,1)S(1)}, bf16[128,512]{0,1:T(8,128)(2,1)S(1)}, u32[]{:S(2)}, u32[]{:S(2)}) collective-permute-start(bf16[128,512]{0,1:T(8,128)(2,1)S(1)} %get-tuple-element.1145), channel_id=1, source_target_pairs={{8,0},{16,8},{24,16},{32,24},{40,32},{48,40},{56,48},{64,56},{72,6... | collective-permute-start | bytes 393224 | tf_op jit(solution)/shard_map/while/body/eval_jaxpr/ppermute | solution.py:19
  764.4 10.1 %collective-permute-start.2 = (bf16[128,512]{0,1:T(8,128)(2,1)S(1)}, bf16[128,512]{0,1:T(8,128)(2,1)S(1)}, u32[]{:S(2)}, u32[]{:S(2)}) collective-permute-start(bf16[128,512]{0,1:T(8,128)(2,1)S(1)} %get-tuple-element.1145), channel_id=1, source_target_pairs={{8,0},{16,8},{24,16},{32,24},{40,32},{48,40},{56,48},{64,56},{72,6... | collective-permute-start | bytes 393224 | tf_op jit(solution)/shard_map/while/body/eval_jaxpr/ppermute | solution.py:19
  775.5 10.1 %collective-permute-start.2 = (bf16[128,512]{0,1:T(8,128)(2,1)S(1)}, bf16[128,512]{0,1:T(8,128)(2,1)S(1)}, u32[]{:S(2)}, u32[]{:S(2)}) collective-permute-start(bf16[128,512]{0,1:T(8,128)(2,1)S(1)} %get-tuple-element.1145), channel_id=1, source_target_pairs={{8,0},{16,8},{24,16},{32,24},{40,32},{48,40},{56,48},{64,56},{72,6... | collective-permute-start | bytes 393224 | tf_op jit(solution)/shard_map/while/body/eval_jaxpr/ppermute | solution.py:19
  786.5 10.1 %collective-permute-start.2 = (bf16[128,512]{0,1:T(8,128)(2,1)S(1)}, bf16[128,512]{0,1:T(8,128)(2,1)S(1)}, u32[]{:S(2)}, u32[]{:S(2)}) collective-permute-start(bf16[128,512]{0,1:T(8,128)(2,1)S(1)} %get-tuple-element.1145), channel_id=1, source_target_pairs={{8,0},{16,8},{24,16},{32,24},{40,32},{48,40},{56,48},{64,56},{72,6... | collective-permute-start | bytes 393224 | tf_op jit(solution)/shard_map/while/body/eval_jaxpr/ppermute | solution.py:19
  797.6 10.1 %collective-permute-start.2 = (bf16[128,512]{0,1:T(8,128)(2,1)S(1)}, bf16[128,512]{0,1:T(8,128)(2,1)S(1)}, u32[]{:S(2)}, u32[]{:S(2)}) collective-permute-start(bf16[128,512]{0,1:T(8,128)(2,1)S(1)} %get-tuple-element.1145), channel_id=1, source_target_pairs={{8,0},{16,8},{24,16},{32,24},{40,32},{48,40},{56,48},{64,56},{72,6... | collective-permute-start | bytes 393224 | tf_op jit(solution)/shard_map/while/body/eval_jaxpr/ppermute | solution.py:19
  808.7 10.1 %collective-permute-start.2 = (bf16[128,512]{0,1:T(8,128)(2,1)S(1)}, bf16[128,512]{0,1:T(8,128)(2,1)S(1)}, u32[]{:S(2)}, u32[]{:S(2)}) collective-permute-start(bf16[128,512]{0,1:T(8,128)(2,1)S(1)} %get-tuple-element.1145), channel_id=1, source_target_pairs={{8,0},{16,8},{24,16},{32,24},{40,32},{48,40},{56,48},{64,56},{72,6... | collective-permute-start | bytes 393224 | tf_op jit(solution)/shard_map/while/body/eval_jaxpr/ppermute | solution.py:19
  819.7 10.1 %collective-permute-start.2 = (bf16[128,512]{0,1:T(8,128)(2,1)S(1)}, bf16[128,512]{0,1:T(8,128)(2,1)S(1)}, u32[]{:S(2)}, u32[]{:S(2)}) collective-permute-start(bf16[128,512]{0,1:T(8,128)(2,1)S(1)} %get-tuple-element.1145), channel_id=1, source_target_pairs={{8,0},{16,8},{24,16},{32,24},{40,32},{48,40},{56,48},{64,56},{72,6... | collective-permute-start | bytes 393224 | tf_op jit(solution)/shard_map/while/body/eval_jaxpr/ppermute | solution.py:19
  (83 other events, 2435.8 us)
where the time goes:
time: 839 us; the launch traced here: 833 us
  starting transfers between devices  333 us (40%)
  waiting for transfers between devices  139 us (17%)
  local copies, waits for them, and re-layouts  117 us (14%)
  blocking collectives  107 us (13%)
  matrix products  55.2 us (7%)
  loops' own time  48.2 us (6%)
  other arithmetic  32.9 us (4%)
    ppermute x124, starting transfers between devices, passed_along(): lax.ppermute(value, axis, [(source, source + steps) for source in range(f...  333 us
    ppermute x124, waiting for transfers between devices, passed_along(): lax.ppermute(value, axis, [(source, source + steps) for source in range(f...  139 us
    psum x1, blocking collectives, per_device(): lax.psum((jnp.sum(upstream_norm * normal, axis=0), jnp.sum(upstream_norm,...  107 us
    dynamic_update_slice x62, local copies, waits for them, and re-layouts, per_device(): lax.scan(key_step, ((key_local, value_local), attended), distances)  40.9 us
    dynamic_slice x62, local copies, waits for them, and re-layouts, per_device(): lax.scan(key_step, ((key_local, value_local), attended), distances)  36.5 us
    dynamic_slice x31, local copies, waits for them, and re-layouts, per_device(): lax.scan(back_step, ((query_local, upstream), grad_query, grad_key, grad_...  30.6 us
    another operation x1, loops' own time, per_device(): lax.scan(back_step, ((query_local, upstream), grad_query, grad_key, grad_...  25.6 us
    another operation x1, loops' own time, per_device(): lax.scan(key_step, ((key_local, value_local), attended), distances)  22.6 us
  transfers between devices with their start and end apart: 124, of which 61 were waited for; matrix products, arithmetic and copies ran while one was open for 14% of the time, Pallas kernels for 0%

commit v1 on v0

v1 whole, which is shorter than its diff:
```python
import math

import jax
import jax.numpy as jnp
from jax import lax
from jax.experimental import pallas as pl
from jax.experimental.pallas import tpu as pltpu
from jax.sharding import PartitionSpec as P

MESH = pl.DeviceIdType.MESH
NX = 4
NY = 8
HD = 128
EPS = 1e-05
USERS = 5

F32 = jnp.float32
BF16 = jnp.bfloat16


def dot(a, b):
    return lax.dot_general(a, b, (((1,), (0,)), ((), ())), preferred_element_type=F32)


def dot_t(a, b):
    return lax.dot_general(a, b, (((1,), (1,)), ((), ())), preferred_element_type=F32)


def make_kernel(nz, rows):
    pairs = NY // 2
    halves = pairs // 2
    stripe = 2 * NY
    heads = NY // 2
    width = heads * HD
    tile_q = 2 * rows
    tile_k = 4 * rows
    scale = HD ** (-0.5)
    norm_scale = 1.0 / math.sqrt(nz * NX * stripe * rows)

    def kernel(
        lengths, q_ref, k_ref, v_ref, gates_ref, cot_ref, gain_ref, bias_ref,
        gq_ref, gk_ref, gv_ref, gg_ref, gn_ref,
        qbuf, kvbuf, probs, derivs, att_acc, att_out, att_in, up, dabuf, q_t, da_t,
        dq_out, dq_in, dk_t, keep, sib_out, sib_in, x_out, x_in, fin, gk_in, gv_in,
        ysum, xsum, csum, zsum,
        q_s, q_r, k_s, k_r, v_s, v_r, f_s, f_r, att_s, att_r, da_s, da_r, dq_s, dq_r,
        sib_s, sib_r, xo_s, xo_r, fk_s, fk_r, fv_s, fv_r,
        ys_s, ys_r, xs_s, xs_r, cs_s, cs_r, zs_s, zs_r,
    ):
        me = lax.axis_index("seq")
        z = lax.axis_index("dp")
        x = me // stripe
        y = (me % stripe) // 2
        c = me % 2
        head = y // 2
        par = y % 2
        mine = y // 2

        def at(xx, yy, cc):
            return {"seq": (xx * NY + yy) * 2 + cc}

        sibling = at(x, y, 1 - c)

        def copy(src, dst, send, recv, target):
            return pltpu.make_async_remote_copy(
                src_ref=src, dst_ref=dst, send_sem=send, recv_sem=recv,
                device_id=target, device_id_type=MESH,
            )

        def arrived(dst, send, recv):
            copy(dst, dst, send, recv, sibling).wait_recv()

        def sent(src, send, recv):
            copy(src, src, send, recv, sibling).wait_send()

        def cols(h):
            return pl.ds(pl.multiple_of(h * HD, HD), HD)

        barrier = pltpu.get_barrier_semaphore()
        partners = [at(x, (y + d) % NY, c) for d in range(1, NY)]
        partners += [at((x + d) % NX, y, c) for d in range(1, NX)]
        partners += [sibling]
        partners += [{"dp": (z + d) % nz} for d in range(1, nz)]
        for partner in partners:
            pl.semaphore_signal(barrier, inc=1, device_id=partner, device_id_type=MESH)
        pl.semaphore_wait(barrier, len(partners))

        kvbuf[0, mine, c, :, 0:HD] = k_ref[:, cols(head)]
        kvbuf[0, mine, c, :, HD:2 * HD] = v_ref[:, cols(head)]
        for d in range(2, NY, 2):
            yy = (y + d) % NY
            copy(
                k_ref.at[:, cols(yy // 2)], kvbuf.at[0, mine, c, :, pl.ds(0, HD)],
                k_s.at[d // 2], k_r.at[mine], at(x, yy, c),
            ).start()
            copy(
                v_ref.at[:, cols(yy // 2)], kvbuf.at[0, mine, c, :, pl.ds(HD, HD)],
                v_s.at[d // 2], v_r.at[mine], at(x, yy, c),
            ).start()
        for d in range(1, NY):
            yy = (y + d) % NY
            copy(
                q_ref.at[:, cols(yy // 2)], qbuf.at[y], q_s.at[d], q_r.at[y], at(x, yy, c)
            ).start()
        qbuf[y] = q_ref[:, cols(head)]

        def forward_block(k):
            block = kvbuf.at[0, k, c]
            copy(block, block, f_s.at[0, k], f_r.at[0, k], sibling).start()

            @pl.when(x < NX - 1)
            def _():
                copy(block, kvbuf.at[1, k, c], f_s.at[1, k], f_r.at[1, k], at((x + 1) % NX, y, c)).start()

            @pl.when(x < NX - 2)
            def _():
                copy(block, kvbuf.at[2, k, c], f_s.at[2, k], f_r.at[2, k], at((x + 2) % NX, y, c)).start()

        forward_block(mine)
        for d in range(1, pairs):
            k = (mine + d) % pairs
            arrived(kvbuf.at[0, k, c, :, pl.ds(0, HD)], k_s.at[0], k_r.at[k])
            arrived(kvbuf.at[0, k, c, :, pl.ds(HD, HD)], v_s.at[0], v_r.at[k])
            forward_block(k)

        ends = []
        running = jnp.int32(0)
        for u in range(USERS):
            running = running + lengths[u]
            ends.append(running)

        def begin_of(block):
            begin = jnp.int32(0)
            last = jnp.int32(0)
            for end in ends:
                begin = jnp.maximum(begin, jnp.where(end <= block, end, 0))
                last = jnp.maximum(last, jnp.where(end == block + 1, 1, 0))
            return begin, last

        row = lax.broadcasted_iota(jnp.int32, (tile_q, 1), 0)
        second = row >= rows
        column = lax.broadcasted_iota(jnp.int32, (1, tile_k), 1)
        column = (column // (2 * rows)) * (4 * rows) + column % (2 * rows)

        def forward_body(t, m, half):
            first = stripe * x + c + 4 * m
            begin0, last0 = begin_of(first)
            begin1, last1 = begin_of(first + 2)
            begin = jnp.where(second, begin1, begin0) * rows
            at_key = column + (stripe * (x - t) + 2 * par + 8 * half) * rows
            allowed = at_key >= begin
            if t == 0:
                at_query = row + jnp.where(second, rows, 0) + first * rows
                last = jnp.where(second, last1, last0)
                start = jnp.where(second, first + 2, first) * rows
                limit = jnp.where(last == 1, start - 1, at_query)
                allowed = allowed & ((at_key <= limit) | (at_key == at_query))
            queries = qbuf[pl.ds(2 * m, 2)].reshape(tile_q, HD)
            keys = kvbuf[t, pl.ds(2 * half, 2), :, :, 0:HD].reshape(tile_k, HD)
            vals = kvbuf[t, pl.ds(2 * half, 2), :, :, HD:2 * HD].reshape(tile_k, HD)
            small = dot_t(queries, keys) * (0.5 * scale)
            up1 = jnp.tanh(small) + 1.0
            prob = small * up1
            deriv = (up1 + prob * (2.0 - up1)) * (0.5 * scale)
            prob = jnp.where(allowed, prob, 0.0).astype(BF16)
            slot = (t * pairs + m) * halves + half
            probs[slot] = prob
            derivs[slot] = jnp.where(allowed, deriv, 0.0).astype(BF16)
            att_acc[m] += dot(prob, vals)

        def spans(t, m):
            if t == 0:
                return 0, m // 2 + 1
            if t == 1:
                return 0, halves
            return m // 2, halves

        def sweep(t, body, first=0, last=pairs):
            def step(m, _):
                low, high = spans(t, m)
                lax.fori_loop(low, high, lambda half, _: body(t, m, half), None)

            lax.fori_loop(first, last, step, None)

        att_acc[...] = jnp.zeros_like(att_acc)
        for d in range(1, NY):
            slot = (y + d) % NY
            arrived(qbuf.at[slot], q_s.at[0], q_r.at[slot])
        for k in range(pairs):
            arrived(kvbuf.at[0, k, 1 - c], f_s.at[0, k], f_r.at[0, k])
        sweep(0, forward_body)

        for t in (1, 2):
            @pl.when(x >= t)
            def _(t=t):
                for k in range(pairs):
                    block = kvbuf.at[t, k, c]
                    arrived(block, f_s.at[t, k], f_r.at[t, k])
                    copy(block, block, f_s.at[t + 2, k], f_r.at[t + 2, k], sibling).start()
                for k in range(pairs):
                    arrived(kvbuf.at[t, k, 1 - c], f_s.at[t + 2, k], f_r.at[t + 2, k])
                sweep(t, forward_body)

        def to_owner(slot, source, landing, send, recv):
            there = landing.at[par, :, cols(head)]

            @pl.when(slot == y)
            def _():
                landing[par, :, cols(head)] = source[slot]

            @pl.when(slot != y)
            def _():
                copy(source.at[slot], there, send.at[slot], recv.at[y], at(x, slot, c)).start()

        for m in range(pairs):
            att_out[2 * m] = att_acc[m, 0:rows].astype(BF16)
            att_out[2 * m + 1] = att_acc[m, rows:2 * rows].astype(BF16)
            to_owner(2 * m, att_out, att_in, att_s, att_r)
            to_owner(2 * m + 1, att_out, att_in, att_s, att_r)

        for m in range(pairs):
            q_t[m] = qbuf[2 * m:2 * m + 2].reshape(tile_q, HD).T

        def gather_owner(landing, send, recv):
            for d in range(1, NY):
                yy = (y + d) % NY
                arrived(landing.at[yy % 2, :, cols(yy // 2)], send.at[0], recv.at[yy])

        gather_owner(att_in, att_s, att_r)
        attended = att_in[0].astype(F32) + att_in[1].astype(F32)
        mean = jnp.mean(attended, axis=-1, keepdims=True)
        centered = attended - mean
        variance = jnp.mean(centered * centered, axis=-1, keepdims=True)
        inverse = lax.rsqrt(variance + EPS)
        normal = centered * inverse
        gain = gain_ref[...]
        cot = cot_ref[...].astype(F32)
        upstream = cot * gates_ref[...].astype(F32)
        dnormal = upstream * gain
        grad_att = inverse * (
            dnormal
            - jnp.mean(dnormal, axis=-1, keepdims=True)
            - normal * jnp.mean(dnormal * normal, axis=-1, keepdims=True)
        )
        up[...] = grad_att.astype(BF16)
        for d in range(1, NY):
            yy = (y + d) % NY
            copy(up.at[:, cols(yy // 2)], dabuf.at[y], da_s.at[d], da_r.at[y], at(x, yy, c)).start()
        dabuf[y] = up[:, cols(head)]
        gg_ref[...] = (cot * (normal * gain + bias_ref[...])).astype(BF16)
        ysum[y, 0:1] = jnp.sum(upstream * normal, axis=0, keepdims=True)
        ysum[y, 1:2] = jnp.sum(upstream, axis=0, keepdims=True)

        def spread(buf, index, count, send, recv, target):
            for d in range(1, count):
                copy(buf.at[index], buf.at[index], send.at[d], recv.at[index], target(d)).start()

        def total(buf, index, count, send, recv):
            for d in range(1, count):
                other = (index + d) % count
                arrived(buf.at[other], send.at[0], recv.at[other])
            result = buf[0]
            for i in range(1, count):
                result = result + buf[i]
            return result

        spread(ysum, y, NY, ys_s, ys_r, lambda d: at(x, (y + d) % NY, c))

        att_acc[...] = jnp.zeros_like(att_acc)
        for d in range(1, NY):
            slot = (y + d) % NY
            arrived(dabuf.at[slot], da_s.at[0], da_r.at[slot])
        for m in range(pairs):
            da_t[m] = dabuf[2 * m:2 * m + 2].reshape(tile_q, HD).T

        def backward_body(t, m, half):
            slot = (t * pairs + m) * halves + half
            ups = dabuf[pl.ds(2 * m, 2)].reshape(tile_q, HD)
            keys = kvbuf[t, pl.ds(2 * half, 2), :, :, 0:HD].reshape(tile_k, HD)
            vals = kvbuf[t, pl.ds(2 * half, 2), :, :, HD:2 * HD].reshape(tile_k, HD)
            grads = (dot_t(ups, vals) * derivs[slot].astype(F32)).astype(BF16)
            att_acc[m] += dot(grads, keys)
            dk_t[half, 0:HD] += dot(q_t[m], grads)
            dk_t[half, HD:2 * HD] += dot(da_t[m], probs[slot])

        def split_cores(t):
            for k in range(pairs):
                part = dk_t[k // 2, :, (k % 2) * 2 * rows:(k % 2 + 1) * 2 * rows].T
                upper, lower = part[0:rows], part[rows:2 * rows]

                @pl.when(c == 0)
                def _(k=k, upper=upper, lower=lower):
                    keep[t, k] = upper
                    sib_out[t, k] = lower.astype(BF16)

                @pl.when(c == 1)
                def _(k=k, upper=upper, lower=lower):
                    keep[t, k] = lower
                    sib_out[t, k] = upper.astype(BF16)

            copy(sib_out.at[t], sib_in.at[t], sib_s.at[t], sib_r.at[t], sibling).start()

        def send_back(t):
            arrived(sib_in.at[t], sib_s.at[t], sib_r.at[t])
            x_out[t - 1] = (keep[t] + sib_in[t].astype(F32)).astype(BF16)
            copy(
                x_out.at[t - 1], x_in.at[t - 1], xo_s.at[t - 1], xo_r.at[t - 1],
                at((x + NX - t) % NX, y, c),
            ).start()

        @pl.when(x >= 2)
        def _():
            dk_t[...] = jnp.zeros_like(dk_t)
            sweep(2, backward_body)
            split_cores(2)

        @pl.when(x >= 1)
        def _():
            dk_t[...] = jnp.zeros_like(dk_t)
            sweep(1, backward_body, 0, pairs // 2)

        @pl.when(x >= 2)
        def _():
            send_back(2)

        @pl.when(x >= 1)
        def _():
            sweep(1, backward_body, pairs // 2, pairs)
            split_cores(1)

        xsum[x] = total(ysum, y, NY, ys_s, ys_r)
        spread(xsum, x, NX, xs_s, xs_r, lambda d: at((x + d) % NX, y, c))

        dk_t[...] = jnp.zeros_like(dk_t)
        sweep(0, backward_body, 0, pairs // 2)

        @pl.when(x >= 1)
        def _():
            send_back(1)

        def dq_pair(m):
            dq_out[2 * m] = att_acc[m, 0:rows].astype(BF16)
            dq_out[2 * m + 1] = att_acc[m, rows:2 * rows].astype(BF16)
            to_owner(2 * m, dq_out, dq_in, dq_s, dq_r)
            to_owner(2 * m + 1, dq_out, dq_in, dq_s, dq_r)

        for m in range(pairs // 2):
            dq_pair(m)
        sweep(0, backward_body, pairs // 2, pairs)
        split_cores(0)
        for m in range(pairs // 2, pairs):
            dq_pair(m)

        csum[c] = total(xsum, x, NX, xs_s, xs_r)
        spread(csum, c, 2, cs_s, cs_r, lambda d: sibling)

        arrived(sib_in.at[0], sib_s.at[0], sib_r.at[0])
        keep[0] = keep[0] + sib_in[0].astype(F32)
        for t in (1, 2):
            @pl.when(x < NX - t)
            def _(t=t):
                arrived(x_in.at[t - 1], xo_s.at[t - 1], xo_r.at[t - 1])
                keep[0] = keep[0] + x_in[t - 1].astype(F32)
        fin[...] = keep[0].astype(BF16)
        for d in range(1, pairs):
            k = (mine + d) % pairs
            yy = par + 2 * k
            copy(fin.at[k, :, pl.ds(0, HD)], gk_in.at[:, cols(head)], fk_s.at[d], fk_r.at[head], at(x, yy, c)).start()
            copy(fin.at[k, :, pl.ds(HD, HD)], gv_in.at[:, cols(head)], fv_s.at[d], fv_r.at[head], at(x, yy, c)).start()
        gk_in[:, cols(head)] = fin[mine, :, 0:HD]
        gv_in[:, cols(head)] = fin[mine, :, HD:2 * HD]

        zsum[z] = total(csum, c, 2, cs_s, cs_r)
        spread(zsum, z, nz, zs_s, zs_r, lambda d: {"dp": (z + d) % nz})

        gather_owner(dq_in, dq_s, dq_r)
        gq_ref[...] = (dq_in[0].astype(F32) + dq_in[1].astype(F32)).astype(BF16)
        for d in range(1, heads):
            h = (head + d) % heads
            arrived(gk_in.at[:, cols(h)], fk_s.at[0], fk_r.at[h])
            arrived(gv_in.at[:, cols(h)], fv_s.at[0], fv_r.at[h])
        gk_ref[...] = gk_in[...]
        gv_ref[...] = gv_in[...]
        gn_ref[...] = total(zsum, z, nz, zs_s, zs_r) * norm_scale

        for d in range(2, NY, 2):
            sent(k_ref.at[:, cols(head)], k_s.at[d // 2], k_r.at[0])
            sent(v_ref.at[:, cols(head)], v_s.at[d // 2], v_r.at[0])
        for d in range(1, NY):
            sent(qbuf.at[0], q_s.at[d], q_r.at[0])
            sent(dabuf.at[0], da_s.at[d], da_r.at[0])
            slot = (y + d) % NY
            sent(att_out.at[slot], att_s.at[slot], att_r.at[0])
            sent(dq_out.at[slot], dq_s.at[slot], dq_r.at[0])
            sent(ysum.at[y], ys_s.at[d], ys_r.at[0])
        for k in range(pairs):
            sent(kvbuf.at[0, k, c], f_s.at[0, k], f_r.at[0, k])
        for t in (1, 2):
            @pl.when(x < NX - t)
            def _(t=t):
                for k in range(pairs):
                    sent(kvbuf.at[0, k, c], f_s.at[t, k], f_r.at[0, k])

            @pl.when(x >= t)
            def _(t=t):
                for k in range(pairs):
                    sent(kvbuf.at[t, k, c], f_s.at[t + 2, k], f_r.at[0, k])
                sent(sib_out.at[t], sib_s.at[t], sib_r.at[t])
                sent(x_out.at[t - 1], xo_s.at[t - 1], xo_r.at[t - 1])
        sent(sib_out.at[0], sib_s.at[0], sib_r.at[0])
        for d in range(1, pairs):
            k = (mine + d) % pairs
            sent(fin.at[k, :, pl.ds(0, HD)], fk_s.at[d], fk_r.at[0])
            sent(fin.at[k, :, pl.ds(HD, HD)], fv_s.at[d], fv_r.at[0])
        for d in range(1, NX):
            sent(xsum.at[x], xs_s.at[d], xs_r.at[0])
        sent(csum.at[c], cs_s.at[1], cs_r.at[0])
        for d in range(1, nz):
            sent(zsum.at[z], zs_s.at[d], zs_r.at[0])

    vm = pltpu.VMEM
    sem = pltpu.SemaphoreType.DMA
    scratch = [
        vm((NY, rows, HD), BF16),
        vm((3, pairs, 2, rows, 2 * HD), BF16),
        vm((3 * pairs * halves, tile_q, tile_k), BF16),
        vm((3 * pairs * halves, tile_q, tile_k), BF16),
        vm((pairs, tile_q, HD), F32),
        vm((NY, rows, HD), BF16),
        vm((2, rows, width), BF16),
        vm((rows, width), BF16),
        vm((NY, rows, HD), BF16),
        vm((pairs, HD, tile_q), BF16),
        vm((pairs, HD, tile_q), BF16),
        vm((NY, rows, HD), BF16),
        vm((2, rows, width), BF16),
        vm((halves, 2 * HD, tile_k), F32),
        vm((3, pairs, rows, 2 * HD), F32),
        vm((3, pairs, rows, 2 * HD), BF16),
        vm((3, pairs, rows, 2 * HD), BF16),
        vm((2, pairs, rows, 2 * HD), BF16),
        vm((2, pairs, rows, 2 * HD), BF16),
        vm((pairs, rows, 2 * HD), BF16),
        vm((rows, width), BF16),
        vm((rows, width), BF16),
        vm((NY, 2, width), F32),
        vm((NX, 2, width), F32),
        vm((2, 2, width), F32),
        vm((nz, 2, width), F32),
        sem((NY,)), sem((NY,)),
        sem((pairs,)), sem((pairs,)), sem((pairs,)), sem((pairs,)),
        sem((5, pairs)), sem((5, pairs)),
        sem((NY,)), sem((NY,)), sem((NY,)), sem((NY,)), sem((NY,)), sem((NY,)),
        sem((3,)), sem((3,)), sem((2,)), sem((2,)),
        sem((pairs,)), sem((pairs,)), sem((pairs,)), sem((pairs,)),
        sem((NY,)), sem((NY,)), sem((NX,)), sem((NX,)), sem((2,)), sem((2,)), sem((nz,)), sem((nz,)),
    ]
    out = jax.ShapeDtypeStruct((rows, width), BF16)
    whole = pl.BlockSpec(memory_space=pltpu.VMEM)
    return pl.pallas_call(
        kernel,
        out_shape=[out, out, out, out, jax.ShapeDtypeStruct((2, width), F32)],
        in_specs=[pl.BlockSpec(memory_space=pltpu.SMEM)] + [whole] * 7,
        out_specs=[whole] * 5,
        scratch_shapes=scratch,
        compiler_params=pltpu.CompilerParams(
            collective_id=0, has_side_effects=True, vmem_limit_bytes=40 * 1024 * 1024
        ),
    )


def solution(mesh):
    nz = mesh.shape["dp"]

    def per_device(queries, keys, values, gates, cotangent, lengths, gain, bias):
        gq, gk, gv, gg, gn = make_kernel(nz, queries.shape[1])(
            lengths[0], queries[0], keys[0], values[0], gates[0], cotangent[0], gain[None], bias[None]
        )
        return gq[None], gk[None], gv[None], gg[None], gn[0], gn[1]

    rows = P("dp", "seq", None)
    return jax.shard_map(
        per_device,
        mesh=mesh,
        in_specs=(rows, rows, rows, rows, rows, P("dp", None), P(), P()),
        out_specs=(rows, rows, rows, rows, P(), P()),
        check_vma=False,
    )
```

time: 839 us -> 96.1 us (0.11)
  the two profiles are of different devices: /device:TPU:3 before, /device:TPU:50 now
where the time goes in v1:
time: 96.1 us; the launch traced here: 95.8 us
  Pallas kernels  86.7 us (90%)
  local copies, waits for them, and re-layouts  8.4 us (9%)
    pallas_call x1, Pallas kernels, per_device(): make_kernel(nz, queries.shape[1])  86.7 us
    unnamed x20, local copies, waits for them, and re-layouts  7.81 us

profile of v1, /device:TPU:50, one launch (start us, length us, event | category | flops | bytes accessed | tf_op | source)
XLA Modules:
  0.0 95.8 jit_solution(10081817205393289309)
XLA Ops:
  0.6 0.0 copy-start.6
  0.6 0.0 copy-start.5
  0.7 0.0 copy-start.7
  0.7 0.7 copy-done.6
  1.3 0.0 copy-done.5
  1.3 0.0 copy-done.7
  1.3 0.0 copy-start
  1.3 0.9 copy-done
  2.2 0.0 copy-start.1
  2.2 0.9 copy-done.1
  3.1 0.0 copy-start.2
  3.1 0.9 copy-done.2
  4.1 0.0 copy-start.3
  4.1 0.9 copy-done.3
  5.0 0.0 copy-start.4
  5.0 0.9 copy-done.4
  5.9 86.7 %shard_map.127 = (bf16[128,512]{1,0:T(8,128)(2,1)S(1)}, bf16[128,512]{1,0:T(8,128)(2,1)S(1)}, bf16[128,512]{1,0:T(8,128)(2,1)S(1)}, bf16[128,512]{1,0:T(8,128)(2,1)S(1)}, f32[2,512]{1,0:T(2,128)S(1)}) custom-call(s32[5]{0:T(128)S(1)} %bitcast.25, bf16[128,512]{1,0:T(8,128)(2,1)S(1)} %bitcast.18, bf16[128,512]{1,0:T(8,128)(2,1)S(1)} %bitcast.19, ...), custom_call_target="tpu_custom_call" | custom-call | tf_op jit(solution)/shard_map/pallas_call | solution.py:476
  92.6 0.6 fusion
  93.2 0.7 copy.18
  93.9 0.7 copy.19
  94.5 0.7 copy.20
  95.2 0.7 copy.21
Async XLA Ops:
  0.6 0.7 copy-start.6
  0.6 0.7 copy-start.5
  0.7 0.7 copy-start.7
  1.3 0.9 copy-start
  2.2 0.9 copy-start.1
  3.1 0.9 copy-start.2
  4.1 0.9 copy-start.3
  5.0 0.9 copy-start.4

commit v2 on v1

v2 whole, which is shorter than its diff:
```python
import math

import jax
import jax.numpy as jnp
from jax import lax
from jax.experimental import pallas as pl
from jax.experimental.pallas import tpu as pltpu
from jax.sharding import PartitionSpec as P

MESH = pl.DeviceIdType.MESH
NX = 4
NY = 8
HD = 128
EPS = 1e-05
USERS = 5

F32 = jnp.float32
BF16 = jnp.bfloat16


def dot(a, b):
    return lax.dot_general(a, b, (((1,), (0,)), ((), ())), preferred_element_type=F32)


def dot_t(a, b):
    return lax.dot_general(a, b, (((1,), (1,)), ((), ())), preferred_element_type=F32)


def make_kernel(nz, rows):
    pairs = NY // 2
    halves = pairs // 2
    stripe = 2 * NY
    heads = NY // 2
    width = heads * HD
    tile_q = 2 * rows
    tile_k = 4 * rows
    scale = HD ** (-0.5)
    norm_scale = 1.0 / math.sqrt(nz * NX * stripe * rows)

    def kernel(
        lengths, q_ref, k_ref, v_ref, gates_ref, cot_ref, gain_ref, bias_ref,
        gq_ref, gk_ref, gv_ref, gg_ref, gn_ref,
        qbuf, kvbuf, gates, cots, probs, derivs, att_acc, att_out, att_in, up, dabuf, q_t, da_t,
        dq_acc, dq_out, dq_in, dk_t, keep, sib_out, sib_in, x_out, x_in, fin, gk_in, gv_in,
        ysum, xsum, csum, zsum, gq_out, gg_out, gn_out, marks,
        own_s, q_s, q_r, k_s, k_r, v_s, v_r, f_s, f_r, att_s, att_r, da_s, da_r, dq_s, dq_r,
        sib_s, sib_r, xo_s, xo_r, fk_s, fk_r, fv_s, fv_r,
        ys_s, ys_r, xs_s, xs_r, cs_s, cs_r, zs_s, zs_r, gn_r, out_s,
    ):
        me = lax.axis_index("seq")
        z = lax.axis_index("dp")
        x = me // stripe
        y = (me % stripe) // 2
        c = me % 2
        head = y // 2
        par = y % 2
        mine = y // 2

        def at(xx, yy, cc):
            return {"seq": (xx * NY + yy) * 2 + cc}

        sibling = at(x, y, 1 - c)

        def copy(src, dst, send, recv, target):
            return pltpu.make_async_remote_copy(
                src_ref=src, dst_ref=dst, send_sem=send, recv_sem=recv,
                device_id=target, device_id_type=MESH,
            )

        def arrived(dst, send, recv):
            copy(dst, dst, send, recv, sibling).wait_recv()

        def sent(src, send, recv):
            copy(src, src, send, recv, sibling).wait_send()

        def cols(h):
            return pl.ds(pl.multiple_of(h * HD, HD), HD)

        own = [
            pltpu.make_async_copy(k_ref.at[:, cols(head)], kvbuf.at[0, mine, c, :, pl.ds(0, HD)], own_s.at[0]),
            pltpu.make_async_copy(v_ref.at[:, cols(head)], kvbuf.at[0, mine, c, :, pl.ds(HD, HD)], own_s.at[1]),
            pltpu.make_async_copy(q_ref.at[:, cols(head)], qbuf.at[y], own_s.at[2]),
            pltpu.make_async_copy(gates_ref, gates, own_s.at[3]),
            pltpu.make_async_copy(cot_ref, cots, own_s.at[4]),
        ]
        for one in own:
            one.start()

        def store(index, here, there):
            pltpu.make_async_copy(here, there, out_s.at[index]).start()

        barrier = pltpu.get_barrier_semaphore()
        partners = [at(x, (y + d) % NY, c) for d in range(1, NY)]
        partners += [at((x + d) % NX, y, c) for d in range(1, NX)]
        partners += [sibling]
        for partner in partners:
            pl.semaphore_signal(barrier, inc=1, device_id=partner, device_id_type=MESH)

        @pl.when(z == 0)
        def _():
            for d in range(1, nz):
                pl.semaphore_signal(barrier, inc=1, device_id={"dp": d}, device_id_type=MESH)

        pl.semaphore_wait(barrier, len(partners) + jnp.where(z == 0, 0, 1))

        for d in range(2, NY, 2):
            yy = (y + d) % NY
            copy(
                k_ref.at[:, cols(yy // 2)], kvbuf.at[0, mine, c, :, pl.ds(0, HD)],
                k_s.at[d // 2], k_r.at[mine], at(x, yy, c),
            ).start()
            copy(
                v_ref.at[:, cols(yy // 2)], kvbuf.at[0, mine, c, :, pl.ds(HD, HD)],
                v_s.at[d // 2], v_r.at[mine], at(x, yy, c),
            ).start()
        def send_queries():
            for d in range(1, NY):
                yy = (y + d) % NY
                copy(
                    q_ref.at[:, cols(yy // 2)], qbuf.at[y], q_s.at[d], q_r.at[y], at(x, yy, c)
                ).start()

        pl.when(y >= NY // 2)(send_queries)

        def forward_block(k, t):
            block = kvbuf.at[0, k, c]

            @pl.when(x < NX - t)
            def _():
                copy(block, kvbuf.at[t, k, c], f_s.at[t, k], f_r.at[t, k], at((x + t) % NX, y, c)).start()

        def share_block(t, k):
            block = kvbuf.at[t, k, c]
            copy(block, block, f_s.at[3 + t, k], f_r.at[3 + t, k], sibling).start()

        def share_stripe(t):
            @pl.when(x >= t)
            def _():
                for k in range(pairs):
                    arrived(kvbuf.at[t, k, c], f_s.at[t, k], f_r.at[t, k])
                    share_block(t, k)

        def shared(t):
            for k in range(pairs):
                arrived(kvbuf.at[t, k, 1 - c], f_s.at[3 + t, k], f_r.at[3 + t, k])

        ends = []
        running = jnp.int32(0)
        for u in range(USERS):
            running = running + lengths[0, u]
            ends.append(running)
        for slot in range(NY):
            block = stripe * x + 2 * slot + c
            begin = jnp.int32(0)
            final = jnp.int32(0)
            for end in ends:
                begin = jnp.maximum(begin, jnp.where(end <= block, end, 0))
                final = jnp.maximum(final, jnp.where(end == block + 1, 1, 0))
            marks[0, slot] = begin * rows
            marks[1, slot] = jnp.where(final == 1, block, 2 * NX * stripe) * rows

        own[0].wait()
        own[1].wait()
        share_block(0, mine)
        forward_block(mine, 1)
        for d in range(1, pairs):
            k = (mine + d) % pairs
            arrived(kvbuf.at[0, k, c, :, pl.ds(0, HD)], k_s.at[0], k_r.at[k])
            arrived(kvbuf.at[0, k, c, :, pl.ds(HD, HD)], v_s.at[0], v_r.at[k])
            share_block(0, k)
            forward_block(k, 1)
        pl.when(y < NY // 2)(send_queries)
        for d in range(pairs):
            forward_block((mine + d) % pairs, 2)
        share_stripe(1)

        column = lax.broadcasted_iota(jnp.int32, (1, tile_k), 1)
        column = (column // (2 * rows)) * (4 * rows) + column % (2 * rows)
        grid_row = lax.broadcasted_iota(jnp.int32, (tile_q, tile_k), 0)
        grid_column = lax.broadcasted_iota(jnp.int32, (tile_q, tile_k), 1)
        grid_gap = (
            (grid_column // (2 * rows)) * (4 * rows) + grid_column % (2 * rows)
            - grid_row - jnp.where(grid_row >= rows, rows, 0)
        )

        def keys_of(t, half):
            return kvbuf[t, 2 * half:2 * half + 2, :, :, 0:HD].reshape(tile_k, HD)

        def values_of(t, half):
            return kvbuf[t, 2 * half:2 * half + 2, :, :, HD:2 * HD].reshape(tile_k, HD)

        def forward_tile(t, m, half):
            shift = (2 * par + 8 * half) * rows
            at_key = column + (stripe * (x - t) * rows + shift)
            inside = []
            for slot in (2 * m, 2 * m + 1):
                kept = at_key >= marks[0, slot]
                if t == 0 and half == m // 2:
                    kept = kept & (at_key < marks[1, slot])
                inside.append(jnp.broadcast_to(jnp.where(kept, 1.0, 0.0), (rows, tile_k)))
            inside = jnp.concatenate(inside, axis=0)
            if t == 0 and half == m // 2:
                gap = grid_gap + (shift - (c + 4 * m) * rows)
                inside = jnp.where(gap < 0, inside, jnp.where(gap == 0, 1.0, 0.0))
            queries = qbuf[2 * m:2 * m + 2].reshape(tile_q, HD)
            small = dot_t(queries, keys_of(t, half)) * (0.5 * scale)
            twice = jnp.tanh(small) + 1.0
            weighed = twice * inside
            prob = small * weighed
            slot = (t * 2 + m // 2) * halves + half
            place = slice((m % 2) * tile_q, (m % 2 + 1) * tile_q)
            prob_low = prob.astype(BF16)
            probs[slot, place] = prob_low
            derivs[slot, place] = (weighed + prob * (2.0 - twice)).astype(BF16)
            return dot(prob_low, values_of(t, half))

        def spans(t, side):
            if t == 0:
                return range(0, side + 1)
            if t == 1:
                return range(0, halves)
            return range(side, halves)

        def forward_side(t, side):
            for m in (2 * side, 2 * side + 1):
                result = None
                for half in spans(t, side):
                    part = forward_tile(t, m, half)
                    result = part if result is None else result + part
                att_acc[m] = result if t == 0 else att_acc[m] + result

        def to_owner(slot, source, landing, send, recv):
            there = landing.at[par, :, cols(head)]

            @pl.when(slot == y)
            def _():
                landing[par, :, cols(head)] = source[slot]

            @pl.when(slot != y)
            def _():
                copy(source.at[slot], there, send.at[slot], recv.at[y], at(x, slot, c)).start()

        def attended_side(side):
            for m in (2 * side, 2 * side + 1):
                att_out[2 * m] = att_acc[m, 0:rows].astype(BF16)
                to_owner(2 * m, att_out, att_in, att_s, att_r)
                att_out[2 * m + 1] = att_acc[m, rows:2 * rows].astype(BF16)
                to_owner(2 * m + 1, att_out, att_in, att_s, att_r)

        def queries_here(side):
            for slot in range(4 * side, 4 * side + 4):
                @pl.when(slot == y)
                def _():
                    own[2].wait()

                @pl.when(slot != y)
                def _(slot=slot):
                    arrived(qbuf.at[slot], q_s.at[0], q_r.at[slot])

        queries_here(1)
        shared(0)
        forward_side(0, 1)

        @pl.when(x >= 1)
        def _():
            shared(1)
            forward_side(1, 1)

        queries_here(0)
        forward_side(0, 0)
        share_stripe(2)

        @pl.when(x >= 2)
        def _():
            shared(2)
            forward_side(2, 1)

        attended_side(1)

        @pl.when(x >= 1)
        def _():
            forward_side(1, 0)

        @pl.when(x >= 2)
        def _():
            forward_side(2, 0)

        attended_side(0)

        def transposed(source, target):
            for m in range(pairs):
                block = source[2 * m:2 * m + 2].reshape(tile_q, HD)
                target[m // 2, :, (m % 2) * tile_q:(m % 2 + 1) * tile_q] = block.T

        def gather_owner(landing, send, recv):
            for d in range(1, NY):
                yy = (y + d) % NY
                arrived(landing.at[yy % 2, :, cols(yy // 2)], send.at[0], recv.at[yy])

        dq_acc[...] = jnp.zeros_like(dq_acc)
        transposed(qbuf, q_t)
        own[3].wait()
        own[4].wait()
        gain = gain_ref[...]
        cot = cots[...].astype(F32)
        upstream = cot * gates[...].astype(F32)
        dnormal = upstream * gain
        dnormal_mean = jnp.mean(dnormal, axis=-1, keepdims=True)
        ysum[y, 1:2] = jnp.sum(upstream, axis=0, keepdims=True)

        gather_owner(att_in, att_s, att_r)
        attended = att_in[0].astype(F32) + att_in[1].astype(F32)
        mean = jnp.mean(attended, axis=-1, keepdims=True)
        centered = attended - mean
        variance = jnp.mean(centered * centered, axis=-1, keepdims=True)
        inverse = lax.rsqrt(variance + EPS)
        normal = centered * inverse
        grad_att = inverse * (
            dnormal - dnormal_mean - normal * jnp.mean(dnormal * normal, axis=-1, keepdims=True)
        )
        up[...] = grad_att.astype(BF16)
        for d in range(1, NY):
            yy = (y + d) % NY
            copy(up.at[:, cols(yy // 2)], dabuf.at[y], da_s.at[d], da_r.at[y], at(x, yy, c)).start()
        dabuf[y] = up[:, cols(head)]
        ysum[y, 0:1] = jnp.sum(upstream * normal, axis=0, keepdims=True)

        def spread(buf, index, count, send, recv, target):
            for d in range(1, count):
                copy(buf.at[index], buf.at[index], send.at[d], recv.at[index], target(d)).start()

        def total(buf, index, count, send, recv):
            for d in range(1, count):
                other = (index + d) % count
                arrived(buf.at[other], send.at[0], recv.at[other])
            result = buf[0]
            for i in range(1, count):
                result = result + buf[i]
            return result

        spread(ysum, y, NY, ys_s, ys_r, lambda d: at(x, (y + d) % NY, c))
        gg_out[...] = (cot * (normal * gain + bias_ref[...])).astype(BF16)
        store(3, gg_out, gg_ref)

        for d in range(1, NY):
            slot = (y + d) % NY
            arrived(dabuf.at[slot], da_s.at[0], da_r.at[slot])
        transposed(dabuf, da_t)

        def backward_tile(t, side, half, fresh):
            slot = (t * 2 + side) * halves + half
            ups = dabuf[4 * side:4 * side + 4].reshape(2 * tile_q, HD)
            pressure = dot_t(ups, values_of(t, half))
            grads = (pressure * derivs[slot].astype(F32)).astype(BF16)
            dq_acc[side] += dot(grads, keys_of(t, half))
            part_k = dot(q_t[side], grads)
            part_v = dot(da_t[side], probs[slot])
            if fresh:
                dk_t[t, half, 0:HD] = part_k
                dk_t[t, half, HD:2 * HD] = part_v
            else:
                dk_t[t, half, 0:HD] += part_k
                dk_t[t, half, HD:2 * HD] += part_v

        def split_cores(t, half):
            for k in (2 * half, 2 * half + 1):
                there = slice((k % 2) * 2 * rows, (k % 2 + 1) * 2 * rows)
                part = jnp.concatenate(
                    [(dk_t[t, half, 0:HD, there] * (0.5 * scale)).T, dk_t[t, half, HD:2 * HD, there].T], axis=1
                )
                upper, lower = part[0:rows], part[rows:2 * rows]

                @pl.when(c == 0)
                def _(k=k, upper=upper, lower=lower):
                    keep[t, k] = upper
                    sib_out[t, k] = lower.astype(BF16)

                @pl.when(c == 1)
                def _(k=k, upper=upper, lower=lower):
                    keep[t, k] = lower
                    sib_out[t, k] = upper.astype(BF16)

            some = pl.ds(2 * half, 2)
            copy(sib_out.at[t, some], sib_in.at[t, some], sib_s.at[t, half], sib_r.at[t, half], sibling).start()

        def send_back(t, half):
            some = pl.ds(2 * half, 2)
            arrived(sib_in.at[t, some], sib_s.at[t, half], sib_r.at[t, half])
            x_out[t - 1, some] = (keep[t, some] + sib_in[t, some].astype(F32)).astype(BF16)
            copy(
                x_out.at[t - 1, some], x_in.at[t - 1, some], xo_s.at[t - 1, half], xo_r.at[t - 1, half],
                at((x + NX - t) % NX, y, c),
            ).start()

        def grad_queries_side(side):
            for m in (2 * side, 2 * side + 1):
                first = (m % 2) * tile_q
                part = dq_acc[side, first:first + rows] * (0.5 * scale)
                dq_out[2 * m] = part.astype(BF16)
                to_owner(2 * m, dq_out, dq_in, dq_s, dq_r)
                part = dq_acc[side, first + rows:first + 2 * rows] * (0.5 * scale)
                dq_out[2 * m + 1] = part.astype(BF16)
                to_owner(2 * m + 1, dq_out, dq_in, dq_s, dq_r)

        @pl.when(x >= 2)
        def _():
            backward_tile(2, 0, 0, True)
            split_cores(2, 0)
            backward_tile(2, 0, 1, True)
            backward_tile(2, 1, 1, False)
            split_cores(2, 1)

        xsum[x] = total(ysum, y, NY, ys_s, ys_r)
        spread(xsum, x, NX, xs_s, xs_r, lambda d: at((x + d) % NX, y, c))

        @pl.when(x >= 2)
        def _():
            send_back(2, 0)

        @pl.when(x >= 1)
        def _():
            backward_tile(1, 0, 0, True)
            backward_tile(1, 1, 0, False)
            split_cores(1, 0)

        @pl.when(x >= 2)
        def _():
            send_back(2, 1)

        @pl.when(x >= 1)
        def _():
            backward_tile(1, 0, 1, True)
            backward_tile(1, 1, 1, False)
            split_cores(1, 1)
            send_back(1, 0)

        backward_tile(0, 0, 0, True)
        grad_queries_side(0)

        @pl.when(x >= 1)
        def _():
            send_back(1, 1)

        backward_tile(0, 1, 0, False)
        split_cores(0, 0)
        backward_tile(0, 1, 1, True)
        split_cores(0, 1)
        grad_queries_side(1)

        csum[c] = total(xsum, x, NX, xs_s, xs_r)
        spread(csum, c, 2, cs_s, cs_r, lambda d: sibling)

        for half in range(halves):
            some = pl.ds(2 * half, 2)
            arrived(sib_in.at[0, some], sib_s.at[0, half], sib_r.at[0, half])
            keep[0, some] = keep[0, some] + sib_in[0, some].astype(F32)

        zsum[z] = total(csum, c, 2, cs_s, cs_r)

        @pl.when(z > 0)
        def _():
            copy(zsum.at[z], zsum.at[z], zs_s.at[0], zs_r.at[z], {"dp": 0}).start()

        for half in range(halves):
            some = pl.ds(2 * half, 2)
            for t in (1, 2):
                @pl.when(x < NX - t)
                def _(t=t, some=some, half=half):
                    arrived(x_in.at[t - 1, some], xo_s.at[t - 1, half], xo_r.at[t - 1, half])
                    keep[0, some] = keep[0, some] + x_in[t - 1, some].astype(F32)
            fin[some] = keep[0, some].astype(BF16)
            for k in (2 * half, 2 * half + 1):
                yy = par + 2 * k

                @pl.when(k == mine)
                def _(k=k):
                    gk_in[:, cols(head)] = fin[k, :, 0:HD]
                    gv_in[:, cols(head)] = fin[k, :, HD:2 * HD]

                @pl.when(k != mine)
                def _(k=k, yy=yy):
                    copy(fin.at[k, :, pl.ds(0, HD)], gk_in.at[:, cols(head)], fk_s.at[k], fk_r.at[head], at(x, yy, c)).start()
                    copy(fin.at[k, :, pl.ds(HD, HD)], gv_in.at[:, cols(head)], fv_s.at[k], fv_r.at[head], at(x, yy, c)).start()

        gather_owner(dq_in, dq_s, dq_r)
        gq_out[...] = (dq_in[0].astype(F32) + dq_in[1].astype(F32)).astype(BF16)
        store(0, gq_out, gq_ref)

        @pl.when(z == 0)
        def _():
            result = zsum[0]
            for i in range(1, nz):
                arrived(zsum.at[i], zs_s.at[0], zs_r.at[i])
                result = result + zsum[i]
            gn_out[...] = result * norm_scale
            for i in range(1, nz):
                copy(gn_out, gn_out, zs_s.at[i], gn_r.at[0], {"dp": i}).start()

        for d in range(2, NY, 2):
            sent(k_ref.at[:, cols(head)], k_s.at[d // 2], k_r.at[0])
            sent(v_ref.at[:, cols(head)], v_s.at[d // 2], v_r.at[0])
        for d in range(1, NY):
            sent(qbuf.at[0], q_s.at[d], q_r.at[0])
            sent(dabuf.at[0], da_s.at[d], da_r.at[0])
            slot = (y + d) % NY
            sent(att_out.at[slot], att_s.at[slot], att_r.at[0])
            sent(dq_out.at[slot], dq_s.at[slot], dq_r.at[0])
            sent(ysum.at[y], ys_s.at[d], ys_r.at[0])
        for k in range(pairs):
            sent(kvbuf.at[0, k, c], f_s.at[3, k], f_r.at[0, k])
        for t in (1, 2):
            @pl.when(x < NX - t)
            def _(t=t):
                for k in range(pairs):
                    sent(kvbuf.at[0, k, c], f_s.at[t, k], f_r.at[0, k])

            @pl.when(x >= t)
            def _(t=t):
                for k in range(pairs):
                    sent(kvbuf.at[t, k, c], f_s.at[3 + t, k], f_r.at[0, k])
                for half in range(halves):
                    some = pl.ds(2 * half, 2)
                    sent(sib_out.at[t, some], sib_s.at[t, half], sib_r.at[t, half])
                    sent(x_out.at[t - 1, some], xo_s.at[t - 1, half], xo_r.at[t - 1, half])
        for half in range(halves):
            some = pl.ds(2 * half, 2)
            sent(sib_out.at[0, some], sib_s.at[0, half], sib_r.at[0, half])
        for d in range(1, NX):
            sent(xsum.at[x], xs_s.at[d], xs_r.at[0])
        sent(csum.at[c], cs_s.at[1], cs_r.at[0])

        @pl.when(z > 0)
        def _():
            sent(zsum.at[z], zs_s.at[0], zs_r.at[0])

        @pl.when(z == 0)
        def _():
            for i in range(1, nz):
                sent(gn_out, zs_s.at[i], zs_r.at[0])

        for d in range(1, heads):
            h = (head + d) % heads
            arrived(gk_in.at[:, cols(h)], fk_s.at[0], fk_r.at[h])
            arrived(gv_in.at[:, cols(h)], fv_s.at[0], fv_r.at[h])
        store(1, gk_in, gk_ref)
        store(2, gv_in, gv_ref)

        @pl.when(z > 0)
        def _():
            arrived(gn_out, zs_s.at[0], gn_r.at[0])

        store(4, gn_out, gn_ref)
        for d in range(1, pairs):
            k = (mine + d) % pairs
            sent(fin.at[k, :, pl.ds(0, HD)], fk_s.at[k], fk_r.at[0])
            sent(fin.at[k, :, pl.ds(HD, HD)], fv_s.at[k], fv_r.at[0])
        for i, (here, there) in enumerate(
            [(gq_out, gq_ref), (gk_in, gk_ref), (gv_in, gv_ref), (gg_out, gg_ref), (gn_out, gn_ref)]
        ):
            pltpu.make_async_copy(here, there, out_s.at[i]).wait()

    vm = pltpu.VMEM
    sem = pltpu.SemaphoreType.DMA
    scratch = [
        vm((NY, rows, HD), BF16),
        vm((3, pairs, 2, rows, 2 * HD), BF16),
        vm((rows, width), BF16),
        vm((rows, width), BF16),
        vm((6 * halves, 2 * tile_q, tile_k), BF16),
        vm((6 * halves, 2 * tile_q, tile_k), BF16),
        vm((pairs, tile_q, HD), F32),
        vm((NY, rows, HD), BF16),
        vm((2, rows, width), BF16),
        vm((rows, width), BF16),
        vm((NY, rows, HD), BF16),
        vm((2, HD, 2 * tile_q), BF16),
        vm((2, HD, 2 * tile_q), BF16),
        vm((2, 2 * tile_q, HD), F32),
        vm((NY, rows, HD), BF16),
        vm((2, rows, width), BF16),
        vm((3, halves, 2 * HD, tile_k), F32),
        vm((3, pairs, rows, 2 * HD), F32),
        vm((3, pairs, rows, 2 * HD), BF16),
        vm((3, pairs, rows, 2 * HD), BF16),
        vm((2, pairs, rows, 2 * HD), BF16),
        vm((2, pairs, rows, 2 * HD), BF16),
        vm((pairs, rows, 2 * HD), BF16),
        vm((rows, width), BF16),
        vm((rows, width), BF16),
        vm((NY, 2, width), F32),
        vm((NX, 2, width), F32),
        vm((2, 2, width), F32),
        vm((nz, 2, width), F32),
        vm((rows, width), BF16),
        vm((rows, width), BF16),
        vm((2, width), F32),
        pltpu.SMEM((2, NY), jnp.int32),
        sem((5,)),
        sem((NY,)), sem((NY,)),
        sem((pairs,)), sem((pairs,)), sem((pairs,)), sem((pairs,)),
        sem((6, pairs)), sem((6, pairs)),
        sem((NY,)), sem((NY,)), sem((NY,)), sem((NY,)), sem((NY,)), sem((NY,)),
        sem((3, halves)), sem((3, halves)), sem((2, halves)), sem((2, halves)),
        sem((pairs,)), sem((pairs,)), sem((pairs,)), sem((pairs,)),
        sem((NY,)), sem((NY,)), sem((NX,)), sem((NX,)), sem((2,)), sem((2,)), sem((nz,)), sem((nz,)), sem((1,)),
        sem((5,)),
    ]
    out = jax.ShapeDtypeStruct((rows, width), BF16)
    whole = pl.BlockSpec(memory_space=pltpu.VMEM)
    far = pl.BlockSpec(memory_space=pltpu.HBM)
    return pl.pallas_call(
        kernel,
        out_shape=[out, out, out, out, jax.ShapeDtypeStruct((2, width), F32)],
        in_specs=[pl.BlockSpec(memory_space=pltpu.SMEM)] + [far] * 5 + [whole] * 2,
        out_specs=[far] * 5,
        scratch_shapes=scratch,
        compiler_params=pltpu.CompilerParams(
            collective_id=0, has_side_effects=True, vmem_limit_bytes=63 * 1024 * 1024
        ),
    )


def write_out(*refs):
    arrays, outs, held, sems = refs[0:5], refs[5:11], refs[11:16], refs[16]
    loads = [pltpu.make_async_copy(arrays[i], held[i], sems.at[i]) for i in range(5)]
    places = list(held[0:4]) + [held[4].at[0], held[4].at[1]]
    stores = [pltpu.make_async_copy(places[i], outs[i], sems.at[5 + i]) for i in range(6)]
    for load in loads:
        load.start()
    for i in range(4):
        loads[i].wait()
        stores[i].start()
    loads[4].wait()
    stores[4].start()
    stores[5].start()
    for store in stores:
        store.wait()


def written(*arrays):
    far = pl.BlockSpec(memory_space=pltpu.HBM)
    gn = arrays[4]
    row = jax.ShapeDtypeStruct(gn.shape[1:], gn.dtype)
    return pl.pallas_call(
        write_out,
        out_shape=[jax.ShapeDtypeStruct(one.shape, one.dtype) for one in arrays[0:4]] + [row, row],
        in_specs=[far] * 5,
        out_specs=[far] * 6,
        scratch_shapes=[pltpu.VMEM(one.shape, one.dtype) for one in arrays] + [pltpu.SemaphoreType.DMA((11,))],
        compiler_params=pltpu.CompilerParams(vmem_limit_bytes=63 * 1024 * 1024),
    )(*arrays)


def solution(mesh):
    nz = mesh.shape["dp"]

    def per_device(queries, keys, values, gates, cotangent, lengths, gain, bias):
        gq, gk, gv, gg, gn = make_kernel(nz, queries.shape[1])(
            lengths, queries[0], keys[0], values[0], gates[0], cotangent[0], gain[None], bias[None]
        )
        gq, gk, gv, gg, gain_grad, bias_grad = written(gq, gk, gv, gg, gn)
        return gq[None], gk[None], gv[None], gg[None], gain_grad, bias_grad

    rows = P("dp", "seq", None)
    return jax.shard_map(
        per_device,
        mesh=mesh,
        in_specs=(rows, rows, rows, rows, rows, P("dp", None), P(), P()),
        out_specs=(rows, rows, rows, rows, P(), P()),
        check_vma=False,
    )
```

time: 96.1 us -> 76.9 us (0.80)
  the two profiles are of different devices: /device:TPU:50 before, /device:TPU:21 now
where the time goes in v2:
time: 76.9 us; the launch traced here: 76.7 us
  Pallas kernels  75.9 us (99%)
  between operations  0.8 us (1%)
    pallas_call x1, Pallas kernels, per_device(): make_kernel(nz, queries.shape[1])  74.1 us
    pallas_call x1, Pallas kernels, written(): pl.pallas_call(write_out, out_shape=[jax.ShapeDtypeStruct(one.shape, one....  1.85 us

profile of v2, /device:TPU:21, one launch (start us, length us, event | category | flops | bytes accessed | tf_op | source)
XLA Modules:
  0.0 76.7 jit_solution(7429175988511866221)
XLA Ops:
  0.6 74.1 %shard_map.127 = (bf16[128,512]{1,0:T(8,128)(2,1)}, bf16[128,512]{1,0:T(8,128)(2,1)}, bf16[128,512]{1,0:T(8,128)(2,1)}, bf16[128,512]{1,0:T(8,128)(2,1)}, f32[2,512]{1,0:T(2,128)}) custom-call(s32[1,5]{1,0:T(1,128)} %lengths.1, bf16[128,512]{1,0:T(8,128)(2,1)} %bitcast.11, bf16[128,512]{1,0:T(8,128)(2,1)} %bitcast.12, bf16[128,512]{1,0:T(8,128)(2,1)} %bitcast.13, ...), custom_call_target="tpu_custom_call" | custom-call | tf_op jit(solution)/shard_map/pallas_call | solution.py:658
  74.7 1.9 %shard_map.128 = (bf16[128,512]{1,0:T(8,128)(2,1)}, bf16[128,512]{1,0:T(8,128)(2,1)}, bf16[128,512]{1,0:T(8,128)(2,1)}, bf16[128,512]{1,0:T(8,128)(2,1)}, f32[512]{0:T(512)}, /*index=5*/f32[512]{0:T(512)}) custom-call(bf16[128,512]{1,0:T(8,128)(2,1)} %get-tuple-element.17.refs_0_, bf16[128,512]{1,0:T(8,128)(2,1)} %get-tuple-element.18.refs_1_, ...), custom_call_target="tpu_custom_call" | custom-call | tf_op jit(solution)/shard_map/pallas_call | solution.py:644

commit v3 on v2

--- a/solution.py
+++ b/solution.py
@@ -41,9 +41,9 @@
         lengths, q_ref, k_ref, v_ref, gates_ref, cot_ref, gain_ref, bias_ref,
         gq_ref, gk_ref, gv_ref, gg_ref, gn_ref,
         qbuf, kvbuf, gates, cots, probs, derivs, att_acc, att_out, att_in, up, dabuf, q_t, da_t,
-        dq_acc, dq_out, dq_in, dk_t, keep, sib_out, sib_in, x_out, x_in, fin, gk_in, gv_in,
-        ysum, xsum, csum, zsum, gq_out, gg_out, gn_out, marks,
-        own_s, q_s, q_r, k_s, k_r, v_s, v_r, f_s, f_r, att_s, att_r, da_s, da_r, dq_s, dq_r,
+        dq_acc, dq_out, dq_in, dk_t, keep, sib_out, sib_in, x_out, x_in, fin,
+        ysum, xsum, csum, zsum, gq_out, gg_out, gn_out, gains, biases, relay, mid_in, pass_in, marks, counts,
+        own_s, r_s, r_r, mid_r, pass_s, pass_r, q_s, q_r, k_s, k_r, v_s, v_r, f_s, f_r, att_s, att_r, da_s, da_r, dq_s, dq_r,
         sib_s, sib_r, xo_s, xo_r, fk_s, fk_r, fv_s, fv_r,
         ys_s, ys_r, xs_s, xs_r, cs_s, cs_r, zs_s, zs_r, gn_r, out_s,
     ):
@@ -76,12 +76,16 @@
         def cols(h):
             return pl.ds(pl.multiple_of(h * HD, HD), HD)
 
+        far_first = sorted(range(1, NY), key=lambda d: -min(d, NY - d))
         own = [
             pltpu.make_async_copy(k_ref.at[:, cols(head)], kvbuf.at[0, mine, c, :, pl.ds(0, HD)], own_s.at[0]),
             pltpu.make_async_copy(v_ref.at[:, cols(head)], kvbuf.at[0, mine, c, :, pl.ds(HD, HD)], own_s.at[1]),
             pltpu.make_async_copy(q_ref.at[:, cols(head)], qbuf.at[y], own_s.at[2]),
             pltpu.make_async_copy(gates_ref, gates, own_s.at[3]),
             pltpu.make_async_copy(cot_ref, cots, own_s.at[4]),
+            pltpu.make_async_copy(lengths, counts, own_s.at[5]),
+            pltpu.make_async_copy(gain_ref, gains, own_s.at[6]),
+            pltpu.make_async_copy(bias_ref, biases, own_s.at[7]),
         ]
         for one in own:
             one.start()
@@ -103,7 +107,9 @@
 
         pl.semaphore_wait(barrier, len(partners) + jnp.where(z == 0, 0, 1))
 
-        for d in range(2, NY, 2):
+        for d in far_first:
+            if d % 2:
+                continue
             yy = (y + d) % NY
             copy(
                 k_ref.at[:, cols(yy // 2)], kvbuf.at[0, mine, c, :, pl.ds(0, HD)],
@@ -113,21 +119,23 @@
                 v_ref.at[:, cols(yy // 2)], kvbuf.at[0, mine, c, :, pl.ds(HD, HD)],
                 v_s.at[d // 2], v_r.at[mine], at(x, yy, c),
             ).start()
-        def send_queries():
-            for d in range(1, NY):
-                yy = (y + d) % NY
-                copy(
-                    q_ref.at[:, cols(yy // 2)], qbuf.at[y], q_s.at[d], q_r.at[y], at(x, yy, c)
-                ).start()
-
-        pl.when(y >= NY // 2)(send_queries)
-
-        def forward_block(k, t):
+        for d in far_first:
+            yy = (y + d) % NY
+            copy(q_ref.at[:, cols(yy // 2)], qbuf.at[y], q_s.at[d], q_r.at[y], at(x, yy, c)).start()
+
+        def forward_block(k):
             block = kvbuf.at[0, k, c]
 
-            @pl.when(x < NX - t)
+            @pl.when(x < NX - 1)
             def _():
-                copy(block, kvbuf.at[t, k, c], f_s.at[t, k], f_r.at[t, k], at((x + t) % NX, y, c)).start()
+                copy(block, kvbuf.at[1, k, c], f_s.at[1, k], f_r.at[1, k], at((x + 1) % NX, y, c)).start()
+
+            @pl.when((x < NX - 2) & (k % 2 == 1))
+            def _():
+                copy(block, relay.at[k // 2], r_s.at[k // 2], r_r.at[k // 2], at((x + NX - 1) % NX, y, c)).start()
+
+        def forward_again(block, k, target):
+            copy(block, kvbuf.at[2, k, c], f_s.at[2, k], f_r.at[2, k], at(target, y, c)).start()
 
         def share_block(t, k):
             block = kvbuf.at[t, k, c]
@@ -139,15 +147,21 @@
                 for k in range(pairs):
                     arrived(kvbuf.at[t, k, c], f_s.at[t, k], f_r.at[t, k])
                     share_block(t, k)
+                    if t == 1 and k % 2 == 0:
+                        @pl.when(x < NX - 1)
+                        def _(k=k):
+                            forward_again(kvbuf.at[1, k, c], k, (x + 1) % NX)
 
         def shared(t):
             for k in range(pairs):
                 arrived(kvbuf.at[t, k, 1 - c], f_s.at[3 + t, k], f_r.at[3 + t, k])
 
+        for i in (5, 6, 7):
+            own[i].wait()
         ends = []
         running = jnp.int32(0)
         for u in range(USERS):
-            running = running + lengths[0, u]
+            running = running + counts[0, u]
             ends.append(running)
         for slot in range(NY):
             block = stripe * x + 2 * slot + c
@@ -162,16 +176,20 @@
         own[0].wait()
         own[1].wait()
         share_block(0, mine)
-        forward_block(mine, 1)
+        forward_block(mine)
         for d in range(1, pairs):
             k = (mine + d) % pairs
             arrived(kvbuf.at[0, k, c, :, pl.ds(0, HD)], k_s.at[0], k_r.at[k])
             arrived(kvbuf.at[0, k, c, :, pl.ds(HD, HD)], v_s.at[0], v_r.at[k])
             share_block(0, k)
-            forward_block(k, 1)
-        pl.when(y < NY // 2)(send_queries)
-        for d in range(pairs):
-            forward_block((mine + d) % pairs, 2)
+            forward_block(k)
+
+        @pl.when((x == 0) | (x == NX - 1))
+        def _():
+            for i in range(halves):
+                arrived(relay.at[i], r_s.at[i], r_r.at[i])
+                forward_again(relay.at[i], 2 * i + 1, (x + NX - 1) % NX)
+
         share_stripe(1)
 
         column = lax.broadcasted_iota(jnp.int32, (1, tile_k), 1)
@@ -214,17 +232,17 @@
             derivs[slot, place] = (weighed + prob * (2.0 - twice)).astype(BF16)
             return dot(prob_low, values_of(t, half))
 
-        def spans(t, side):
+        def spans(t, m):
             if t == 0:
-                return range(0, side + 1)
+                return range(0, m // 2 + 1)
             if t == 1:
                 return range(0, halves)
-            return range(side, halves)
+            return range(m // 2, halves)
 
         def forward_side(t, side):
-            for m in (2 * side, 2 * side + 1):
+            for m in range(side, pairs, 2):
                 result = None
-                for half in spans(t, side):
+                for half in spans(t, m):
                     part = forward_tile(t, m, half)
                     result = part if result is None else result + part
                 att_acc[m] = result if t == 0 else att_acc[m] + result
@@ -241,7 +259,7 @@
                 copy(source.at[slot], there, send.at[slot], recv.at[y], at(x, slot, c)).start()
 
         def attended_side(side):
-            for m in (2 * side, 2 * side + 1):
+            for m in range(side, pairs, 2):
                 att_out[2 * m] = att_acc[m, 0:rows].astype(BF16)
                 to_owner(2 * m, att_out, att_in, att_s, att_r)
                 att_out[2 * m + 1] = att_acc[m, rows:2 * rows].astype(BF16)
@@ -257,17 +275,18 @@
                 def _(slot=slot):
                     arrived(qbuf.at[slot], q_s.at[0], q_r.at[slot])
 
+        queries_here(0)
         queries_here(1)
         shared(0)
         forward_side(0, 1)
+        forward_side(0, 0)
 
         @pl.when(x >= 1)
         def _():
             shared(1)
             forward_side(1, 1)
-
-        queries_here(0)
-        forward_side(0, 0)
+            forward_side(1, 0)
+
         share_stripe(2)
 
         @pl.when(x >= 2)
@@ -276,10 +295,6 @@
             forward_side(2, 1)
 
         attended_side(1)
-
-        @pl.when(x >= 1)
-        def _():
-            forward_side(1, 0)
 
         @pl.when(x >= 2)
         def _():
@@ -297,11 +312,24 @@
                 yy = (y + d) % NY
                 arrived(landing.at[yy % 2, :, cols(yy // 2)], send.at[0], recv.at[yy])
 
+        def spread(buf, index, count, send, recv, target):
+            for d in range(1, count):
+                copy(buf.at[index], buf.at[index], send.at[d], recv.at[index], target(d)).start()
+
+        def total(buf, index, count, send, recv):
+            for d in range(1, count):
+                other = (index + d) % count
+                arrived(buf.at[other], send.at[0], recv.at[other])
+            result = buf[0]
+            for i in range(1, count):
+                result = result + buf[i]
+            return result
+
         dq_acc[...] = jnp.zeros_like(dq_acc)
         transposed(qbuf, q_t)
         own[3].wait()
         own[4].wait()
-        gain = gain_ref[...]
+        gain = gains[...]
         cot = cots[...].astype(F32)
         upstream = cot * gates[...].astype(F32)
         dnormal = upstream * gain
@@ -319,28 +347,17 @@
             dnormal - dnormal_mean - normal * jnp.mean(dnormal * normal, axis=-1, keepdims=True)
         )
         up[...] = grad_att.astype(BF16)
-        for d in range(1, NY):
+        ysum[y, 0:1] = jnp.sum(upstream * normal, axis=0, keepdims=True)
+        spread(ysum, y, NY, ys_s, ys_r, lambda d: at(x, (y + d) % NY, c))
+        for d in far_first:
             yy = (y + d) % NY
             copy(up.at[:, cols(yy // 2)], dabuf.at[y], da_s.at[d], da_r.at[y], at(x, yy, c)).start()
         dabuf[y] = up[:, cols(head)]
-        ysum[y, 0:1] = jnp.sum(upstream * normal, axis=0, keepdims=True)
-
-        def spread(buf, index, count, send, recv, target):
-            for d in range(1, count):
-                copy(buf.at[index], buf.at[index], send.at[d], recv.at[index], target(d)).start()
-
-        def total(buf, index, count, send, recv):
-            for d in range(1, count):
-                other = (index + d) % count
-                arrived(buf.at[other], send.at[0], recv.at[other])
-            result = buf[0]
-            for i in range(1, count):
-                result = result + buf[i]
-            return result
-
-        spread(ysum, y, NY, ys_s, ys_r, lambda d: at(x, (y + d) % NY, c))
-        gg_out[...] = (cot * (normal * gain + bias_ref[...])).astype(BF16)
+        gg_out[...] = (cot * (normal * gain + biases[...])).astype(BF16)
         store(3, gg_out, gg_ref)
+
+        xsum[x] = total(ysum, y, NY, ys_s, ys_r)
+        spread(xsum, x, NX, xs_s, xs_r, lambda d: at((x + d) % NX, y, c))
 
         for d in range(1, NY):
             slot = (y + d) % NY
@@ -383,13 +400,50 @@
             some = pl.ds(2 * half, 2)
             copy(sib_out.at[t, some], sib_in.at[t, some], sib_s.at[t, half], sib_r.at[t, half], sibling).start()
 
-        def send_back(t, half):
+        turn = mine % 2
+
+        def summed(t, k):
+            return keep[t, k] + sib_in[t, k].astype(F32)
+
+        def sibling_here(t, half):
             some = pl.ds(2 * half, 2)
             arrived(sib_in.at[t, some], sib_s.at[t, half], sib_r.at[t, half])
-            x_out[t - 1, some] = (keep[t, some] + sib_in[t, some].astype(F32)).astype(BF16)
+
+        def back_two(half):
+            sibling_here(2, half)
+            odd = 2 * half + turn
+            even = 2 * half + 1 - turn
+            x_out[1, even] = summed(2, even).astype(BF16)
+            x_out[1, odd] = summed(2, odd).astype(BF16)
+            copy(x_out.at[1, even], mid_in.at[half], xo_s.at[1, even], mid_r.at[half], at((x + NX - 1) % NX, y, c)).start()
+            copy(x_out.at[1, odd], pass_in.at[half], xo_s.at[1, odd], pass_r.at[half], at((x + 1) % NX, y, c)).start()
+
+        def back_one(k):
+            copy(x_out.at[0, k], x_in.at[0, k], xo_s.at[0, k], xo_r.at[0, k], at((x + NX - 1) % NX, y, c)).start()
+
+        def back_odd(half):
+            sibling_here(1, half)
+            odd = 2 * half + turn
+            x_out[0, odd] = summed(1, odd).astype(BF16)
+            back_one(odd)
+
+        def back_even(half):
+            even = 2 * half + 1 - turn
+            keep[1, even] = summed(1, even)
+
+            @pl.when(x < NX - 1)
+            def _():
+                arrived(mid_in.at[half], xo_s.at[1, 0], mid_r.at[half])
+                keep[1, even] += mid_in[half].astype(F32)
+
+            x_out[0, even] = keep[1, even].astype(BF16)
+            back_one(even)
+
+        def pass_back(half):
+            arrived(pass_in.at[half], xo_s.at[1, 0], pass_r.at[half])
             copy(
-                x_out.at[t - 1, some], x_in.at[t - 1, some], xo_s.at[t - 1, half], xo_r.at[t - 1, half],
-                at((x + NX - t) % NX, y, c),
+                pass_in.at[half], x_in.at[1, 2 * half + turn], pass_s.at[half], xo_r.at[1, 2 * half + turn],
+                at((x + 1) % NX, y, c),
             ).start()
 
         def grad_queries_side(side):
@@ -410,12 +464,12 @@
             backward_tile(2, 1, 1, False)
             split_cores(2, 1)
 
-        xsum[x] = total(ysum, y, NY, ys_s, ys_r)
-        spread(xsum, x, NX, xs_s, xs_r, lambda d: at((x + d) % NX, y, c))
+        csum[c] = total(xsum, x, NX, xs_s, xs_r)
+        spread(csum, c, 2, cs_s, cs_r, lambda d: sibling)
 
         @pl.when(x >= 2)
         def _():
-            send_back(2, 0)
+            back_two(0)
 
         @pl.when(x >= 1)
         def _():
@@ -425,66 +479,82 @@
 
         @pl.when(x >= 2)
         def _():
-            send_back(2, 1)
+            back_two(1)
 
         @pl.when(x >= 1)
         def _():
             backward_tile(1, 0, 1, True)
             backward_tile(1, 1, 1, False)
             split_cores(1, 1)
-            send_back(1, 0)
+            back_odd(0)
+
+        zsum[z] = total(csum, c, 2, cs_s, cs_r)
+
+        @pl.when(z > 0)
+        def _():
+            copy(zsum.at[z], zsum.at[z], zs_s.at[0], zs_r.at[z], {"dp": 0}).start()
 
         backward_tile(0, 0, 0, True)
         grad_queries_side(0)
 
         @pl.when(x >= 1)
         def _():
-            send_back(1, 1)
+            back_odd(1)
+            back_even(0)
 
         backward_tile(0, 1, 0, False)
         split_cores(0, 0)
+
+        @pl.when(x >= 1)
+        def _():
+            back_even(1)
+
+        @pl.when(x == NX - 1)
+        def _():
+            for half in range(halves):
+                pass_back(half)
+
         backward_tile(0, 1, 1, True)
         split_cores(0, 1)
         grad_queries_side(1)
 
-        csum[c] = total(xsum, x, NX, xs_s, xs_r)
-        spread(csum, c, 2, cs_s, cs_r, lambda d: sibling)
+        @pl.when(x == 0)
+        def _():
+            for half in range(halves):
+                pass_back(half)
 
         for half in range(halves):
             some = pl.ds(2 * half, 2)
             arrived(sib_in.at[0, some], sib_s.at[0, half], sib_r.at[0, half])
             keep[0, some] = keep[0, some] + sib_in[0, some].astype(F32)
 
-        zsum[z] = total(csum, c, 2, cs_s, cs_r)
-
-        @pl.when(z > 0)
-        def _():
-            copy(zsum.at[z], zsum.at[z], zs_s.at[0], zs_r.at[z], {"dp": 0}).start()
-
-        for half in range(halves):
-            some = pl.ds(2 * half, 2)
-            for t in (1, 2):
-                @pl.when(x < NX - t)
-                def _(t=t, some=some, half=half):
-                    arrived(x_in.at[t - 1, some], xo_s.at[t - 1, half], xo_r.at[t - 1, half])
-                    keep[0, some] = keep[0, some] + x_in[t - 1, some].astype(F32)
-            fin[some] = keep[0, some].astype(BF16)
-            for k in (2 * half, 2 * half + 1):
+        for odd in (1, 0):
+            for half in range(halves):
+                k = (mine + 2 * half + 2 + 1 - odd) % pairs
+
+                @pl.when(x < NX - 1)
+                def _(k=k):
+                    arrived(x_in.at[0, k], xo_s.at[0, k], xo_r.at[0, k])
+                    keep[0, k] += x_in[0, k].astype(F32)
+
+                if odd:
+                    @pl.when(x < NX - 2)
+                    def _(k=k):
+                        arrived(x_in.at[1, k], xo_s.at[1, k], xo_r.at[1, k])
+                        keep[0, k] += x_in[1, k].astype(F32)
+
+                fin[k] = keep[0, k].astype(BF16)
                 yy = par + 2 * k
 
                 @pl.when(k == mine)
                 def _(k=k):
-                    gk_in[:, cols(head)] = fin[k, :, 0:HD]
-                    gv_in[:, cols(head)] = fin[k, :, HD:2 * HD]
+                    pltpu.make_async_copy(fin.at[k, :, pl.ds(0, HD)], gk_ref.at[:, cols(head)], out_s.at[1]).start()
+                    pltpu.make_async_copy(fin.at[k, :, pl.ds(HD, HD)], gv_ref.at[:, cols(head)], out_s.at[2]).start()
 
                 @pl.when(k != mine)
                 def _(k=k, yy=yy):
-                    copy(fin.at[k, :, pl.ds(0, HD)], gk_in.at[:, cols(head)], fk_s.at[k], fk_r.at[head], at(x, yy, c)).start()
-                    copy(fin.at[k, :, pl.ds(HD, HD)], gv_in.at[:, cols(head)], fv_s.at[k], fv_r.at[head], at(x, yy, c)).start()
-
-        gather_owner(dq_in, dq_s, dq_r)
-        gq_out[...] = (dq_in[0].astype(F32) + dq_in[1].astype(F32)).astype(BF16)
-        store(0, gq_out, gq_ref)
+                    copy(fin.at[k, :, pl.ds(0, HD)], gk_ref.at[:, cols(head)], fk_s.at[k], fk_r.at[head], at(x, yy, c)).start()
+                    copy(fin.at[k, :, pl.ds(HD, HD)], gv_ref.at[:, cols(head)], fv_s.at[k], fv_r.at[head], at(x, yy, c)).start()
 
         @pl.when(z == 0)
         def _():
@@ -495,6 +565,11 @@
             gn_out[...] = result * norm_scale
             for i in range(1, nz):
                 copy(gn_out, gn_out, zs_s.at[i], gn_r.at[0], {"dp": i}).start()
+
+        gather_owner(dq_in, dq_s, dq_r)
+        gq_out[...] = (dq_in[0].astype(F32) + dq_in[1].astype(F32)).astype(BF16)
+        store(0, gq_out, gq_ref)
+
 
         for d in range(2, NY, 2):
             sent(k_ref.at[:, cols(head)], k_s.at[d // 2], k_r.at[0])
@@ -508,12 +583,30 @@
             sent(ysum.at[y], ys_s.at[d], ys_r.at[0])
         for k in range(pairs):
             sent(kvbuf.at[0, k, c], f_s.at[3, k], f_r.at[0, k])
+
+        @pl.when(x < NX - 1)
+        def _():
+            for k in range(pairs):
+                sent(kvbuf.at[0, k, c], f_s.at[1, k], f_r.at[0, k])
+
+        @pl.when(x < NX - 2)
+        def _():
+            for i in range(halves):
+                sent(relay.at[i], r_s.at[i], r_r.at[i])
+
+        @pl.when((x == 0) | (x == NX - 1))
+        def _():
+            for half in range(halves):
+                sent(pass_in.at[half], pass_s.at[half], pass_r.at[half])
+            for k in range(1, pairs, 2):
+                sent(kvbuf.at[0, k, c], f_s.at[2, k], f_r.at[0, k])
+
+        @pl.when((x > 0) & (x < NX - 1))
+        def _():
+            for k in range(0, pairs, 2):
+                sent(kvbuf.at[0, k, c], f_s.at[2, k], f_r.at[0, k])
+
         for t in (1, 2):
-            @pl.when(x < NX - t)
-            def _(t=t):
-                for k in range(pairs):
-                    sent(kvbuf.at[0, k, c], f_s.at[t, k], f_r.at[0, k])
-
             @pl.when(x >= t)
             def _(t=t):
                 for k in range(pairs):
@@ -521,7 +614,8 @@
                 for half in range(halves):
                     some = pl.ds(2 * half, 2)
                     sent(sib_out.at[t, some], sib_s.at[t, half], sib_r.at[t, half])
-                    sent(x_out.at[t - 1, some], xo_s.at[t - 1, half], xo_r.at[t - 1, half])
+                for k in range(pairs):
+                    sent(x_out.at[t - 1, k], xo_s.at[t - 1, k], xo_r.at[t - 1, k])
         for half in range(halves):
             some = pl.ds(2 * half, 2)
             sent(sib_out.at[0, some], sib_s.at[0, half], sib_r.at[0, half])
@@ -540,11 +634,8 @@
 
         for d in range(1, heads):
             h = (head + d) % heads
-            arrived(gk_in.at[:, cols(h)], fk_s.at[0], fk_r.at[h])
-            arrived(gv_in.at[:, cols(h)], fv_s.at[0], fv_r.at[h])
-        store(1, gk_in, gk_ref)
-        store(2, gv_in, gv_ref)
-
+            arrived(gk_ref.at[:, cols(h)], fk_s.at[0], fk_r.at[h])
+            arrived(gv_ref.at[:, cols(h)], fv_s.at[0], fv_r.at[h])
         @pl.when(z > 0)
         def _():
             arrived(gn_out, zs_s.at[0], gn_r.at[0])
@@ -555,7 +646,13 @@
             sent(fin.at[k, :, pl.ds(0, HD)], fk_s.at[k], fk_r.at[0])
             sent(fin.at[k, :, pl.ds(HD, HD)], fv_s.at[k], fv_r.at[0])
         for i, (here, there) in enumerate(
-            [(gq_out, gq_ref), (gk_in, gk_ref), (gv_in, gv_ref), (gg_out, gg_ref), (gn_out, gn_ref)]
+            [
+                (gq_out, gq_ref),
+                (fin.at[mine, :, pl.ds(0, HD)], gk_ref.at[:, cols(head)]),
+                (fin.at[mine, :, pl.ds(HD, HD)], gv_ref.at[:, cols(head)]),
+                (gg_out, gg_ref),
+                (gn_out, gn_ref),
+            ]
         ):
             pltpu.make_async_copy(here, there, out_s.at[i]).wait()
 
@@ -585,8 +682,6 @@
         vm((2, pairs, rows, 2 * HD), BF16),
         vm((2, pairs, rows, 2 * HD), BF16),
         vm((pairs, rows, 2 * HD), BF16),
-        vm((rows, width), BF16),
-        vm((rows, width), BF16),
         vm((NY, 2, width), F32),
         vm((NX, 2, width), F32),
         vm((2, 2, width), F32),
@@ -594,24 +689,29 @@
         vm((rows, width), BF16),
         vm((rows, width), BF16),
         vm((2, width), F32),
+        vm((1, width), F32),
+        vm((1, width), F32),
+        vm((halves, rows, 2 * HD), BF16),
+        vm((halves, rows, 2 * HD), BF16),
+        vm((halves, rows, 2 * HD), BF16),
         pltpu.SMEM((2, NY), jnp.int32),
-        sem((5,)),
+        pltpu.SMEM((1, USERS), jnp.int32),
+        sem((8,)), sem((halves,)), sem((halves,)), sem((halves,)), sem((halves,)), sem((halves,)),
         sem((NY,)), sem((NY,)),
         sem((pairs,)), sem((pairs,)), sem((pairs,)), sem((pairs,)),
         sem((6, pairs)), sem((6, pairs)),
         sem((NY,)), sem((NY,)), sem((NY,)), sem((NY,)), sem((NY,)), sem((NY,)),
-        sem((3, halves)), sem((3, halves)), sem((2, halves)), sem((2, halves)),
+        sem((3, halves)), sem((3, halves)), sem((2, pairs)), sem((2, pairs)),
         sem((pairs,)), sem((pairs,)), sem((pairs,)), sem((pairs,)),
         sem((NY,)), sem((NY,)), sem((NX,)), sem((NX,)), sem((2,)), sem((2,)), sem((nz,)), sem((nz,)), sem((1,)),
         sem((5,)),
     ]
     out = jax.ShapeDtypeStruct((rows, width), BF16)
-    whole = pl.BlockSpec(memory_space=pltpu.VMEM)
     far = pl.BlockSpec(memory_space=pltpu.HBM)
     return pl.pallas_call(
         kernel,
         out_shape=[out, out, out, out, jax.ShapeDtypeStruct((2, width), F32)],
-        in_specs=[pl.BlockSpec(memory_space=pltpu.SMEM)] + [far] * 5 + [whole] * 2,
+        in_specs=[far] * 8,
         out_specs=[far] * 5,
         scratch_shapes=scratch,
         compiler_params=pltpu.CompilerParams(

time: 76.9 us -> 72.7 us (0.945)
  the two profiles are of different devices: /device:TPU:21 before, /device:TPU:1 now
where the time goes in v3:
time: 72.7 us; the launch traced here: 72.6 us
  Pallas kernels  71.8 us (99%)
  between operations  0.8 us (1%)
    pallas_call x1, Pallas kernels, per_device(): make_kernel(nz, queries.shape[1])  69.9 us
    pallas_call x1, Pallas kernels, written(): pl.pallas_call(write_out, out_shape=[jax.ShapeDtypeStruct(one.shape, one....  1.85 us

profile of v3, /device:TPU:1, one launch (start us, length us, event | category | flops | bytes accessed | tf_op | source)
XLA Modules:
  0.0 72.6 jit_solution(3731887940597880962)
XLA Ops:
  0.6 69.9 %shard_map.127 = (bf16[128,512]{1,0:T(8,128)(2,1)}, bf16[128,512]{1,0:T(8,128)(2,1)}, bf16[128,512]{1,0:T(8,128)(2,1)}, bf16[128,512]{1,0:T(8,128)(2,1)}, f32[2,512]{1,0:T(2,128)}) custom-call(s32[1,5]{1,0:T(1,128)} %lengths.1, bf16[128,512]{1,0:T(8,128)(2,1)} %bitcast.11, bf16[128,512]{1,0:T(8,128)(2,1)} %bitcast.12, bf16[128,512]{1,0:T(8,128)(2,1)} %bitcast.13, ...), custom_call_target="tpu_custom_call" | custom-call | tf_op jit(solution)/shard_map/pallas_call | solution.py:758
  70.6 1.9 %shard_map.128 = (bf16[128,512]{1,0:T(8,128)(2,1)}, bf16[128,512]{1,0:T(8,128)(2,1)}, bf16[128,512]{1,0:T(8,128)(2,1)}, bf16[128,512]{1,0:T(8,128)(2,1)}, f32[512]{0:T(512)}, /*index=5*/f32[512]{0:T(512)}) custom-call(bf16[128,512]{1,0:T(8,128)(2,1)} %get-tuple-element.17.refs_0_, bf16[128,512]{1,0:T(8,128)(2,1)} %get-tuple-element.18.refs_1_, ...), custom_call_target="tpu_custom_call" | custom-call | tf_op jit(solution)/shard_map/pallas_call | solution.py:744

commit v4 on v3

--- a/solution.py
+++ b/solution.py
@@ -225,8 +225,8 @@
             twice = jnp.tanh(small) + 1.0
             weighed = twice * inside
             prob = small * weighed
-            slot = (t * 2 + m // 2) * halves + half
-            place = slice((m % 2) * tile_q, (m % 2 + 1) * tile_q)
+            slot = (t * 2 + m % 2) * halves + half
+            place = slice((m // 2) * tile_q, (m // 2 + 1) * tile_q)
             prob_low = prob.astype(BF16)
             probs[slot, place] = prob_low
             derivs[slot, place] = (weighed + prob * (2.0 - twice)).astype(BF16)
@@ -258,12 +258,17 @@
             def _():
                 copy(source.at[slot], there, send.at[slot], recv.at[y], at(x, slot, c)).start()
 
+        def to_owners(side, source, landing, send, recv):
+            for far in (1, 0):
+                for i in range(2):
+                    slot = (y // 4 + far) % 2 * 4 + 2 * side + (y + i) % 2
+                    to_owner(slot, source, landing, send, recv)
+
         def attended_side(side):
             for m in range(side, pairs, 2):
                 att_out[2 * m] = att_acc[m, 0:rows].astype(BF16)
-                to_owner(2 * m, att_out, att_in, att_s, att_r)
                 att_out[2 * m + 1] = att_acc[m, rows:2 * rows].astype(BF16)
-                to_owner(2 * m + 1, att_out, att_in, att_s, att_r)
+            to_owners(side, att_out, att_in, att_s, att_r)
 
         def queries_here(side):
             for slot in range(4 * side, 4 * side + 4):
@@ -278,34 +283,37 @@
         queries_here(0)
         queries_here(1)
         shared(0)
+        forward_side(0, 0)
         forward_side(0, 1)
-        forward_side(0, 0)
 
         @pl.when(x >= 1)
         def _():
             shared(1)
+            forward_side(1, 0)
+
+        share_stripe(2)
+
+        @pl.when(x >= 1)
+        def _():
             forward_side(1, 1)
-            forward_side(1, 0)
-
-        share_stripe(2)
 
         @pl.when(x >= 2)
         def _():
             shared(2)
+            forward_side(2, 0)
+
+        attended_side(0)
+
+        @pl.when(x >= 2)
+        def _():
             forward_side(2, 1)
 
         attended_side(1)
-
-        @pl.when(x >= 2)
-        def _():
-            forward_side(2, 0)
-
-        attended_side(0)
 
         def transposed(source, target):
             for m in range(pairs):
                 block = source[2 * m:2 * m + 2].reshape(tile_q, HD)
-                target[m // 2, :, (m % 2) * tile_q:(m % 2 + 1) * tile_q] = block.T
+                target[m % 2, :, (m // 2) * tile_q:(m // 2 + 1) * tile_q] = block.T
 
         def gather_owner(landing, send, recv):
             for d in range(1, NY):
@@ -364,15 +372,17 @@
             arrived(dabuf.at[slot], da_s.at[0], da_r.at[slot])
         transposed(dabuf, da_t)
 
-        def backward_tile(t, side, half, fresh):
+        def backward_tile(t, side, half):
             slot = (t * 2 + side) * halves + half
-            ups = dabuf[4 * side:4 * side + 4].reshape(2 * tile_q, HD)
+            ms = [m for m in (side, side + 2) if half in spans(t, m)]
+            span = slice(ms[0] // 2 * tile_q, (ms[-1] // 2 + 1) * tile_q)
+            ups = jnp.concatenate([dabuf[2 * m:2 * m + 2].reshape(tile_q, HD) for m in ms], axis=0)
             pressure = dot_t(ups, values_of(t, half))
-            grads = (pressure * derivs[slot].astype(F32)).astype(BF16)
-            dq_acc[side] += dot(grads, keys_of(t, half))
-            part_k = dot(q_t[side], grads)
-            part_v = dot(da_t[side], probs[slot])
-            if fresh:
+            grads = (pressure * derivs[slot, span].astype(F32)).astype(BF16)
+            dq_acc[side, span] += dot(grads, keys_of(t, half))
+            part_k = dot(q_t[side, :, span], grads)
+            part_v = dot(da_t[side, :, span], probs[slot, span])
+            if side == 0:
                 dk_t[t, half, 0:HD] = part_k
                 dk_t[t, half, HD:2 * HD] = part_v
             else:
@@ -447,44 +457,39 @@
             ).start()
 
         def grad_queries_side(side):
-            for m in (2 * side, 2 * side + 1):
-                first = (m % 2) * tile_q
+            for m in range(side, pairs, 2):
+                first = (m // 2) * tile_q
                 part = dq_acc[side, first:first + rows] * (0.5 * scale)
                 dq_out[2 * m] = part.astype(BF16)
-                to_owner(2 * m, dq_out, dq_in, dq_s, dq_r)
                 part = dq_acc[side, first + rows:first + 2 * rows] * (0.5 * scale)
                 dq_out[2 * m + 1] = part.astype(BF16)
-                to_owner(2 * m + 1, dq_out, dq_in, dq_s, dq_r)
+            to_owners(side, dq_out, dq_in, dq_s, dq_r)
 
         @pl.when(x >= 2)
         def _():
-            backward_tile(2, 0, 0, True)
-            split_cores(2, 0)
-            backward_tile(2, 0, 1, True)
-            backward_tile(2, 1, 1, False)
-            split_cores(2, 1)
+            for half in range(halves):
+                backward_tile(2, 0, half)
+                backward_tile(2, 1, half)
+                split_cores(2, half)
+            back_two(0)
 
         csum[c] = total(xsum, x, NX, xs_s, xs_r)
         spread(csum, c, 2, cs_s, cs_r, lambda d: sibling)
 
+        @pl.when(x >= 1)
+        def _():
+            backward_tile(1, 0, 0)
+            backward_tile(1, 1, 0)
+            split_cores(1, 0)
+
         @pl.when(x >= 2)
         def _():
-            back_two(0)
+            back_two(1)
 
         @pl.when(x >= 1)
         def _():
-            backward_tile(1, 0, 0, True)
-            backward_tile(1, 1, 0, False)
-            split_cores(1, 0)
-
-        @pl.when(x >= 2)
-        def _():
-            back_two(1)
-
-        @pl.when(x >= 1)
-        def _():
-            backward_tile(1, 0, 1, True)
-            backward_tile(1, 1, 1, False)
+            backward_tile(1, 0, 1)
+            backward_tile(1, 1, 1)
             split_cores(1, 1)
             back_odd(0)
 
@@ -494,7 +499,8 @@
         def _():
             copy(zsum.at[z], zsum.at[z], zs_s.at[0], zs_r.at[z], {"dp": 0}).start()
 
-        backward_tile(0, 0, 0, True)
+        backward_tile(0, 0, 0)
+        backward_tile(0, 0, 1)
         grad_queries_side(0)
 
         @pl.when(x >= 1)
@@ -502,26 +508,24 @@
             back_odd(1)
             back_even(0)
 
-        backward_tile(0, 1, 0, False)
+        @pl.when((x == 0) | (x == NX - 1))
+        def _():
+            pass_back(0)
+
+        backward_tile(0, 1, 0)
         split_cores(0, 0)
 
         @pl.when(x >= 1)
         def _():
             back_even(1)
 
-        @pl.when(x == NX - 1)
-        def _():
-            for half in range(halves):
-                pass_back(half)
-
-        backward_tile(0, 1, 1, True)
+        @pl.when((x == 0) | (x == NX - 1))
+        def _():
+            pass_back(1)
+
+        backward_tile(0, 1, 1)
         split_cores(0, 1)
         grad_queries_side(1)
-
-        @pl.when(x == 0)
-        def _():
-            for half in range(halves):
-                pass_back(half)
 
         for half in range(halves):
             some = pl.ds(2 * half, 2)
@@ -563,8 +567,9 @@
                 arrived(zsum.at[i], zs_s.at[0], zs_r.at[i])
                 result = result + zsum[i]
             gn_out[...] = result * norm_scale
+            store(4, gn_out, gn_ref)
             for i in range(1, nz):
-                copy(gn_out, gn_out, zs_s.at[i], gn_r.at[0], {"dp": i}).start()
+                copy(gn_out, gn_ref, zs_s.at[i], gn_r.at[0], {"dp": i}).start()
 
         gather_owner(dq_in, dq_s, dq_r)
         gq_out[...] = (dq_in[0].astype(F32) + dq_in[1].astype(F32)).astype(BF16)
@@ -638,9 +643,12 @@
             arrived(gv_ref.at[:, cols(h)], fv_s.at[0], fv_r.at[h])
         @pl.when(z > 0)
         def _():
-            arrived(gn_out, zs_s.at[0], gn_r.at[0])
-
-        store(4, gn_out, gn_ref)
+            arrived(gn_ref, zs_s.at[0], gn_r.at[0])
+
+        @pl.when(z == 0)
+        def _():
+            pltpu.make_async_copy(gn_out, gn_ref, out_s.at[4]).wait()
+
         for d in range(1, pairs):
             k = (mine + d) % pairs
             sent(fin.at[k, :, pl.ds(0, HD)], fk_s.at[k], fk_r.at[0])
@@ -651,7 +659,6 @@
                 (fin.at[mine, :, pl.ds(0, HD)], gk_ref.at[:, cols(head)]),
                 (fin.at[mine, :, pl.ds(HD, HD)], gv_ref.at[:, cols(head)]),
                 (gg_out, gg_ref),
-                (gn_out, gn_ref),
             ]
         ):
             pltpu.make_async_copy(here, there, out_s.at[i]).wait()

time: 72.7 us -> 71.3 us (0.981)
  Pallas kernels: 71.8 us -> 69.7 us
    pallas_call x1, Pallas kernels: 69.9 us -> 67.8 us  [per_device(): make_kernel(nz, queries.shape[1])]
where the time goes in v4:
time: 71.3 us; the launch traced here: 70.5 us
  Pallas kernels  69.7 us (98%)
  between operations  0.8 us (1%)
    pallas_call x1, Pallas kernels, per_device(): make_kernel(nz, queries.shape[1])  67.8 us
    pallas_call x1, Pallas kernels, written(): pl.pallas_call(write_out, out_shape=[jax.ShapeDtypeStruct(one.shape, one....  1.85 us

profile of v4, /device:TPU:1, one launch (start us, length us, event | category | flops | bytes accessed | tf_op | source)
XLA Modules:
  0.0 70.5 jit_solution(12142376864740382417)
XLA Ops:
  0.6 67.8 %shard_map.127 = (bf16[128,512]{1,0:T(8,128)(2,1)}, bf16[128,512]{1,0:T(8,128)(2,1)}, bf16[128,512]{1,0:T(8,128)(2,1)}, bf16[128,512]{1,0:T(8,128)(2,1)}, f32[2,512]{1,0:T(2,128)}) custom-call(s32[1,5]{1,0:T(1,128)} %lengths.1, bf16[128,512]{1,0:T(8,128)(2,1)} %bitcast.11, bf16[128,512]{1,0:T(8,128)(2,1)} %bitcast.12, bf16[128,512]{1,0:T(8,128)(2,1)} %bitcast.13, ...), custom_call_target="tpu_custom_call" | custom-call | tf_op jit(solution)/shard_map/pallas_call | solution.py:765
  68.5 1.9 %shard_map.128 = (bf16[128,512]{1,0:T(8,128)(2,1)}, bf16[128,512]{1,0:T(8,128)(2,1)}, bf16[128,512]{1,0:T(8,128)(2,1)}, bf16[128,512]{1,0:T(8,128)(2,1)}, f32[512]{0:T(512)}, /*index=5*/f32[512]{0:T(512)}) custom-call(bf16[128,512]{1,0:T(8,128)(2,1)} %get-tuple-element.17.refs_0_, bf16[128,512]{1,0:T(8,128)(2,1)} %get-tuple-element.18.refs_1_, ...), custom_call_target="tpu_custom_call" | custom-call | tf_op jit(solution)/shard_map/pallas_call | solution.py:751

commit v5 on v4

--- a/solution.py
+++ b/solution.py
@@ -310,8 +310,8 @@
 
         attended_side(1)
 
-        def transposed(source, target):
-            for m in range(pairs):
+        def transposed(source, target, side):
+            for m in range(side, pairs, 2):
                 block = source[2 * m:2 * m + 2].reshape(tile_q, HD)
                 target[m % 2, :, (m // 2) * tile_q:(m // 2 + 1) * tile_q] = block.T
 
@@ -334,7 +334,8 @@
             return result
 
         dq_acc[...] = jnp.zeros_like(dq_acc)
-        transposed(qbuf, q_t)
+        transposed(qbuf, q_t, 0)
+        transposed(qbuf, q_t, 1)
         own[3].wait()
         own[4].wait()
         gain = gains[...]
@@ -367,10 +368,13 @@
         xsum[x] = total(ysum, y, NY, ys_s, ys_r)
         spread(xsum, x, NX, xs_s, xs_r, lambda d: at((x + d) % NX, y, c))
 
-        for d in range(1, NY):
-            slot = (y + d) % NY
-            arrived(dabuf.at[slot], da_s.at[0], da_r.at[slot])
-        transposed(dabuf, da_t)
+        def upstream_here(side):
+            for slot in (2 * side, 2 * side + 1, 2 * side + 4, 2 * side + 5):
+                @pl.when(slot != y)
+                def _(slot=slot):
+                    arrived(dabuf.at[slot], da_s.at[0], da_r.at[slot])
+
+            transposed(dabuf, da_t, side)
 
         def backward_tile(t, side, half):
             slot = (t * 2 + side) * halves + half
@@ -465,32 +469,62 @@
                 dq_out[2 * m + 1] = part.astype(BF16)
             to_owners(side, dq_out, dq_in, dq_s, dq_r)
 
+        upstream_here(0)
+
         @pl.when(x >= 2)
         def _():
             for half in range(halves):
                 backward_tile(2, 0, half)
+
+        @pl.when(x >= 1)
+        def _():
+            for half in range(halves):
+                backward_tile(1, 0, half)
+
+        for half in range(halves):
+            backward_tile(0, 0, half)
+        grad_queries_side(0)
+        upstream_here(1)
+
+        @pl.when(x == 1)
+        def _():
+            for half in range(halves):
+                backward_tile(1, 1, half)
+                split_cores(1, half)
+
+        @pl.when(x <= 1)
+        def _():
+            for half in range(halves):
+                backward_tile(0, 1, half)
+                split_cores(0, half)
+            grad_queries_side(1)
+
+        @pl.when(x >= 2)
+        def _():
+            for half in range(halves):
                 backward_tile(2, 1, half)
                 split_cores(2, half)
-            back_two(0)
 
         csum[c] = total(xsum, x, NX, xs_s, xs_r)
         spread(csum, c, 2, cs_s, cs_r, lambda d: sibling)
 
-        @pl.when(x >= 1)
-        def _():
-            backward_tile(1, 0, 0)
+        @pl.when(x >= 2)
+        def _():
             backward_tile(1, 1, 0)
             split_cores(1, 0)
 
         @pl.when(x >= 2)
         def _():
+            back_two(0)
             back_two(1)
 
-        @pl.when(x >= 1)
-        def _():
-            backward_tile(1, 0, 1)
+        @pl.when(x >= 2)
+        def _():
             backward_tile(1, 1, 1)
             split_cores(1, 1)
+
+        @pl.when(x >= 1)
+        def _():
             back_odd(0)
 
         zsum[z] = total(csum, c, 2, cs_s, cs_r)
@@ -499,9 +533,10 @@
         def _():
             copy(zsum.at[z], zsum.at[z], zs_s.at[0], zs_r.at[z], {"dp": 0}).start()
 
-        backward_tile(0, 0, 0)
-        backward_tile(0, 0, 1)
-        grad_queries_side(0)
+        @pl.when(x >= 2)
+        def _():
+            backward_tile(0, 1, 0)
+            split_cores(0, 0)
 
         @pl.when(x >= 1)
         def _():
@@ -512,20 +547,22 @@
         def _():
             pass_back(0)
 
-        backward_tile(0, 1, 0)
-        split_cores(0, 0)
+        @pl.when(x >= 2)
+        def _():
+            backward_tile(0, 1, 1)
+            split_cores(0, 1)
 
         @pl.when(x >= 1)
         def _():
             back_even(1)
 
+        @pl.when(x >= 2)
+        def _():
+            grad_queries_side(1)
+
         @pl.when((x == 0) | (x == NX - 1))
         def _():
             pass_back(1)
-
-        backward_tile(0, 1, 1)
-        split_cores(0, 1)
-        grad_queries_side(1)
 
         for half in range(halves):
             some = pl.ds(2 * half, 2)

time: 71.3 us -> 69.9 us (0.980)
  the two profiles are of different devices: /device:TPU:1 before, /device:TPU:11 now
where the time goes in v5:
time: 69.9 us; the launch traced here: 69.7 us
  Pallas kernels  68.9 us (99%)
  between operations  0.8 us (1%)
    pallas_call x1, Pallas kernels, per_device(): make_kernel(nz, queries.shape[1])  67.1 us
    pallas_call x1, Pallas kernels, written(): pl.pallas_call(write_out, out_shape=[jax.ShapeDtypeStruct(one.shape, one....  1.85 us

profile of v5, /device:TPU:11, one launch (start us, length us, event | category | flops | bytes accessed | tf_op | source)
XLA Modules:
  0.0 69.7 jit_solution(13405164980982905896)
XLA Ops:
  0.6 67.1 %shard_map.127 = (bf16[128,512]{1,0:T(8,128)(2,1)}, bf16[128,512]{1,0:T(8,128)(2,1)}, bf16[128,512]{1,0:T(8,128)(2,1)}, bf16[128,512]{1,0:T(8,128)(2,1)}, f32[2,512]{1,0:T(2,128)}) custom-call(s32[1,5]{1,0:T(1,128)} %lengths.1, bf16[128,512]{1,0:T(8,128)(2,1)} %bitcast.11, bf16[128,512]{1,0:T(8,128)(2,1)} %bitcast.12, bf16[128,512]{1,0:T(8,128)(2,1)} %bitcast.13, ...), custom_call_target="tpu_custom_call" | custom-call | tf_op jit(solution)/shard_map/pallas_call | solution.py:802
  67.7 1.9 %shard_map.128 = (bf16[128,512]{1,0:T(8,128)(2,1)}, bf16[128,512]{1,0:T(8,128)(2,1)}, bf16[128,512]{1,0:T(8,128)(2,1)}, bf16[128,512]{1,0:T(8,128)(2,1)}, f32[512]{0:T(512)}, /*index=5*/f32[512]{0:T(512)}) custom-call(bf16[128,512]{1,0:T(8,128)(2,1)} %get-tuple-element.17.refs_0_, bf16[128,512]{1,0:T(8,128)(2,1)} %get-tuple-element.18.refs_1_, ...), custom_call_target="tpu_custom_call" | custom-call | tf_op jit(solution)/shard_map/pallas_call | solution.py:788
